TPU v7x, 32 devices: a whole 2x2x4 slice. The times are simulated.
32 devices in a mesh: rep: 16 (over z, x, core), exp: 2 (over y).
Axes of the slice: x: 2, y: 2, z: 4, core: 2. Of those that a mesh axis runs over, the one named last changes fastest.
Arguments:
- tokens: bfloat16 [25216, 384], P(('rep', 'exp')), may hold values from -6 to 6
- routes: int32 [25216, 2], P(('rep', 'exp')), may hold values from 0 to 7, all different within a row; in each aligned block of 788 rows (0 to 787, 788 to 1575, ...) at most 394 rows name the same one
- norm_gains: float32 [4, 384], replicated, may hold values from 0.25 to 1.75
- attn_qkv: bfloat16 [2, 384, 1152], replicated, may hold values from -0.3125 to 0.3125
- attn_out: bfloat16 [2, 384, 384], replicated, may hold values from -1.75 to 1.75
- mlp_in: bfloat16 [384, 1536], replicated, may hold values from -0.3125 to 0.3125
- mlp_out: bfloat16 [1536, 384], replicated, may hold values from -0.3125 to 0.3125
- router: bfloat16 [384, 8], replicated, may hold values from -0.21875 to 0.21875
- experts_in: bfloat16 [8, 384, 1536], P('exp'), may hold values from -0.3125 to 0.3125
- experts_out: bfloat16 [8, 1536, 384], P('exp'), may hold values from -0.3125 to 0.3125
- cotangent: bfloat16 [25216, 384], P(('rep', 'exp')), may hold values from -6 to 6
Outputs:
- activations: bfloat16 [25216, 384], P(('rep', 'exp'))
- input_grad: float32 [25216, 384], P(('rep', 'exp'))
- qkv_grad: float32 [2, 384, 1152], replicated
- proj_grad: float32 [2, 384, 384], replicated
- gain_grad: float32 [4, 384], replicated
- mlp_in_grad: float32 [384, 1536], replicated
- mlp_out_grad: float32 [1536, 384], replicated
- router_grad: float32 [384, 8], replicated
- experts_in_grad: float32 [8, 384, 1536], P('exp', None, 'rep')
- experts_out_grad: float32 [8, 1536, 384], P('exp', 'rep')
Inputs may be any that keep to these rules, and one draw needn't show every extreme that they name: `routes`: each row names 2 different experts; of the 788 rows of one device no expert is named by more than 394 rows, and in every draw some expert is named by exactly 394 rows of some device.
All inputs are finite; a program needn't handle non-finite values.
Results may differ from a plain program's by a relative error of at most 0.025.
Values may be sent and summed in bfloat16 or wider, within the bound.
A program may use at most 320 MiB of HBM per device.

v0:
```python
import jax
import jax.numpy as jnp
from jax import lax
from jax.sharding import PartitionSpec as P

HEADS = 6
PATCHES = 197


eps_norm = 1e-06


def layer_norm(values, norm_gain):
    centred = values - jnp.mean(values, axis=-1, keepdims=True)
    spread = jnp.mean(centred * centred, axis=-1, keepdims=True)
    return centred * lax.rsqrt(spread + eps_norm) * norm_gain


def gelu_exact(values):
    return jax.nn.gelu(values, approximate=False)


def slot_positions(routes, experts, capacity):
    flat_routes = routes.reshape(-1)
    onehot = (flat_routes[:, None] == jnp.arange(experts, dtype=jnp.int32)[None, :]).astype(
        jnp.int32
    )
    before = jnp.cumsum(onehot, axis=0, dtype=jnp.int32) - onehot
    slot_index = jnp.sum(before * onehot, axis=1, dtype=jnp.int32)
    return flat_routes * capacity + slot_index


def split_heads(qkv_rows):
    row_count, triple = qkv_rows.shape
    head_size = triple // (3 * HEADS)
    return qkv_rows.reshape(row_count // PATCHES, PATCHES, 3, HEADS, head_size)


def attend_forward(values, norm_gain, w_qkv, w_out):
    row_count, model_width = values.shape
    score_scale = (model_width // HEADS) ** (-0.5)
    normed = layer_norm(values, norm_gain).astype(jnp.bfloat16)
    qkv_rows = jnp.dot(normed, w_qkv, preferred_element_type=jnp.float32).astype(jnp.bfloat16)
    heads_view = split_heads(qkv_rows)
    scores = (
        jnp.einsum(
            "iqhc,ikhc->ihqk",
            heads_view[:, :, 0],
            heads_view[:, :, 1],
            preferred_element_type=jnp.float32,
        )
        * score_scale
    )
    row_peak = jnp.max(scores, axis=-1, keepdims=True)
    row_total = jnp.sum(jnp.exp(scores - row_peak), axis=-1, keepdims=True)
    shifted = row_peak + jnp.log(row_total)
    soft_weights = jnp.exp(scores - shifted).astype(jnp.bfloat16)
    mixed_heads = jnp.einsum(
        "ihqk,ikhc->iqhc", soft_weights, heads_view[:, :, 2], preferred_element_type=jnp.float32
    )
    mixed_heads = mixed_heads.reshape(row_count, model_width).astype(jnp.bfloat16)
    branch = jnp.dot(mixed_heads, w_out, preferred_element_type=jnp.float32)
    return (values + branch, (values, normed, qkv_rows, shifted, mixed_heads))


def attend_backward(gradient, stored, norm_gain, w_qkv, w_out):
    values, normed, qkv_rows, shifted, mixed_heads = stored
    row_count, model_width = values.shape
    head_size = model_width // HEADS
    score_scale = head_size ** (-0.5)
    grad_branch = gradient.astype(jnp.bfloat16)
    grad_w_out = jnp.dot(mixed_heads.T, grad_branch, preferred_element_type=jnp.float32)
    grad_mixed = jnp.dot(grad_branch, w_out.T, preferred_element_type=jnp.float32).astype(
        jnp.bfloat16
    )
    grad_mixed = grad_mixed.reshape(row_count // PATCHES, PATCHES, HEADS, head_size)
    heads_view = split_heads(qkv_rows)
    queries, key_rows, value_rows = (heads_view[:, :, 0], heads_view[:, :, 1], heads_view[:, :, 2])
    scores = (
        jnp.einsum("iqhc,ikhc->ihqk", queries, key_rows, preferred_element_type=jnp.float32)
        * score_scale
    )
    soft_weights = jnp.exp(scores - shifted)
    grad_value = jnp.einsum(
        "ihqk,iqhc->ikhc",
        soft_weights.astype(jnp.bfloat16),
        grad_mixed,
        preferred_element_type=jnp.float32,
    )
    grad_soft = jnp.einsum(
        "iqhc,ikhc->ihqk", grad_mixed, value_rows, preferred_element_type=jnp.float32
    )
    grad_scores = soft_weights * (
        grad_soft - jnp.sum(soft_weights * grad_soft, axis=-1, keepdims=True)
    )
    grad_scores = grad_scores.astype(jnp.bfloat16)
    grad_query = (
        jnp.einsum("ihqk,ikhc->iqhc", grad_scores, key_rows, preferred_element_type=jnp.float32)
        * score_scale
    )
    grad_key = (
        jnp.einsum("ihqk,iqhc->ikhc", grad_scores, queries, preferred_element_type=jnp.float32)
        * score_scale
    )
    grad_qkv = (
        jnp.stack([grad_query, grad_key, grad_value], axis=2)
        .reshape(row_count, 3 * model_width)
        .astype(jnp.bfloat16)
    )
    grad_w_qkv = jnp.dot(normed.T, grad_qkv, preferred_element_type=jnp.float32)
    grad_normed = jnp.dot(grad_qkv, w_qkv.T, preferred_element_type=jnp.float32)
    grad_values, grad_gain = jax.vjp(layer_norm, values, norm_gain)[1](grad_normed)
    return (gradient + grad_values, grad_gain, grad_w_qkv, grad_w_out)


def dense_forward(values, norm_gain, w_in, w_out):
    normed = layer_norm(values, norm_gain).astype(jnp.bfloat16)
    hidden = jnp.dot(normed, w_in, preferred_element_type=jnp.float32)
    activated = gelu_exact(hidden).astype(jnp.bfloat16)
    branch = jnp.dot(activated, w_out, preferred_element_type=jnp.float32)
    return (values + branch, (values, normed, hidden, activated))


def dense_backward(gradient, stored, norm_gain, w_in, w_out):
    values, normed, hidden, activated = stored
    grad_branch = gradient.astype(jnp.bfloat16)
    grad_w_out = jnp.dot(activated.T, grad_branch, preferred_element_type=jnp.float32)
    grad_act = jnp.dot(grad_branch, w_out.T, preferred_element_type=jnp.float32)
    grad_hidden = jax.vjp(gelu_exact, hidden)[1](grad_act)[0].astype(jnp.bfloat16)
    grad_w_in = jnp.dot(normed.T, grad_hidden, preferred_element_type=jnp.float32)
    grad_normed = jnp.dot(grad_hidden, w_in.T, preferred_element_type=jnp.float32)
    grad_values, grad_gain = jax.vjp(layer_norm, values, norm_gain)[1](grad_normed)
    return (gradient + grad_values, grad_gain, grad_w_in, grad_w_out)


def shards(
    tokens,
    routes,
    norm_gains,
    attn_qkv,
    attn_out,
    mlp_in,
    mlp_out,
    router,
    experts_in,
    experts_out,
    cotangent,
):
    row_count, model_width = tokens.shape
    groups = lax.axis_size("exp")
    local_experts = experts_in.shape[0]
    experts = local_experts * groups
    choices_each = routes.shape[1]
    capacity = 2 * choices_each * row_count // experts
    after_one, stored_one = attend_forward(
        tokens.astype(jnp.float32), norm_gains[0], attn_qkv[0], attn_out[0]
    )
    after_two, stored_two = dense_forward(after_one, norm_gains[1], mlp_in, mlp_out)
    after_three, stored_three = attend_forward(after_two, norm_gains[2], attn_qkv[1], attn_out[1])
    normed_four = layer_norm(after_three, norm_gains[3]).astype(jnp.bfloat16)
    logits = jnp.dot(normed_four, router, preferred_element_type=jnp.float32)
    chosen = (routes[:, :, None] == jnp.arange(experts, dtype=jnp.int32)[None, None, :]).astype(
        jnp.float32
    )
    picked = jnp.sum(logits[:, None, :] * chosen, axis=-1)
    gate_weights = jax.nn.softmax(picked, axis=-1)
    positions = slot_positions(routes, experts, capacity)
    pair_rows = jnp.repeat(normed_four, choices_each, axis=0)
    outgoing = (
        jnp.zeros((experts * capacity, model_width), jnp.bfloat16).at[positions].set(pair_rows)
    )
    outgoing = outgoing.reshape(groups, local_experts, capacity, model_width)
    incoming = lax.all_to_all(outgoing, "exp", split_axis=0, concat_axis=0, tiled=True)
    expert_hidden = jnp.einsum(
        "sicd,idf->sicf", incoming, experts_in, preferred_element_type=jnp.float32
    )
    expert_act = gelu_exact(expert_hidden).astype(jnp.bfloat16)
    expert_out = jnp.einsum(
        "sicf,ifd->sicd", expert_act, experts_out, preferred_element_type=jnp.float32
    ).astype(jnp.bfloat16)
    returned = lax.all_to_all(expert_out, "exp", split_axis=0, concat_axis=0, tiled=True)
    pair_out = returned.reshape(experts * capacity, model_width)[positions].reshape(
        row_count, choices_each, model_width
    )
    pair_out = pair_out.astype(jnp.float32)
    after_four = after_three + jnp.sum(gate_weights[:, :, None] * pair_out, axis=1)
    grad_four = cotangent.astype(jnp.float32)
    grad_pairs = (gate_weights[:, :, None] * grad_four[:, None, :]).astype(jnp.bfloat16)
    grad_gates = jnp.sum(pair_out * grad_four[:, None, :], axis=-1)
    grad_picked = gate_weights * (
        grad_gates - jnp.sum(gate_weights * grad_gates, axis=-1, keepdims=True)
    )
    grad_logits = jnp.sum(chosen * grad_picked[:, :, None], axis=1).astype(jnp.bfloat16)
    grad_router = jnp.dot(normed_four.T, grad_logits, preferred_element_type=jnp.float32)
    grad_normed = jnp.dot(grad_logits, router.T, preferred_element_type=jnp.float32)
    outgoing_grad = (
        jnp.zeros((experts * capacity, model_width), jnp.bfloat16)
        .at[positions]
        .set(grad_pairs.reshape(-1, model_width))
    )
    outgoing_grad = outgoing_grad.reshape(groups, local_experts, capacity, model_width)
    incoming_grad = lax.all_to_all(outgoing_grad, "exp", split_axis=0, concat_axis=0, tiled=True)
    grad_exp_out = jnp.einsum(
        "sicf,sicd->ifd", expert_act, incoming_grad, preferred_element_type=jnp.float32
    )
    grad_exp_act = jnp.einsum(
        "sicd,ifd->sicf", incoming_grad, experts_out, preferred_element_type=jnp.float32
    )
    grad_exp_hidden = jax.vjp(gelu_exact, expert_hidden)[1](grad_exp_act)[0].astype(jnp.bfloat16)
    grad_exp_in = jnp.einsum(
        "sicd,sicf->idf", incoming, grad_exp_hidden, preferred_element_type=jnp.float32
    )
    grad_rows_out = jnp.einsum(
        "sicf,idf->sicd", grad_exp_hidden, experts_in, preferred_element_type=jnp.float32
    ).astype(jnp.bfloat16)
    grad_back = lax.all_to_all(grad_rows_out, "exp", split_axis=0, concat_axis=0, tiled=True)
    grad_pair_rows = grad_back.reshape(experts * capacity, model_width)[positions].reshape(
        row_count, choices_each, model_width
    )
    grad_normed = grad_normed + jnp.sum(grad_pair_rows.astype(jnp.float32), axis=1)
    grad_three_norm, grad_gain_three = jax.vjp(layer_norm, after_three, norm_gains[3])[1](
        grad_normed
    )
    grad_three = grad_four + grad_three_norm
    grad_two, grad_gain_two, grad_qkv_two, grad_proj_two = attend_backward(
        grad_three, stored_three, norm_gains[2], attn_qkv[1], attn_out[1]
    )
    grad_one, grad_gain_one, grad_mlp_in, grad_mlp_out = dense_backward(
        grad_two, stored_two, norm_gains[1], mlp_in, mlp_out
    )
    grad_input, grad_gain_zero, grad_qkv_one, grad_proj_one = attend_backward(
        grad_one, stored_one, norm_gains[0], attn_qkv[0], attn_out[0]
    )
    expert_sums = (
        lax.psum_scatter(
            grad_exp_in.astype(jnp.bfloat16), "rep", scatter_dimension=2, tiled=True
        ).astype(jnp.float32),
        lax.psum_scatter(
            grad_exp_out.astype(jnp.bfloat16), "rep", scatter_dimension=1, tiled=True
        ).astype(jnp.float32),
    )
    shared = lax.psum(
        (
            jnp.stack([grad_qkv_one, grad_qkv_two]),
            jnp.stack([grad_proj_one, grad_proj_two]),
            jnp.stack([grad_gain_zero, grad_gain_one, grad_gain_two, grad_gain_three]),
            grad_mlp_in,
            grad_mlp_out,
            grad_router,
        ),
        ("rep", "exp"),
    )
    qkv_total, proj_total, gain_total, mlp_in_total, mlp_out_total, router_total = shared
    return (
        after_four.astype(jnp.bfloat16),
        grad_input,
        qkv_total,
        proj_total,
        gain_total,
        mlp_in_total,
        mlp_out_total,
        router_total,
        expert_sums[0],
        expert_sums[1],
    )


def solution(mesh):
    return jax.shard_map(
        shards,
        mesh=mesh,
        in_specs=(
            P(("rep", "exp"), None),
            P(("rep", "exp"), None),
            P(),
            P(),
            P(),
            P(),
            P(),
            P(),
            P("exp", None, None),
            P("exp", None, None),
            P(("rep", "exp"), None),
        ),
        out_specs=(
            P(("rep", "exp"), None),
            P(("rep", "exp"), None),
            P(),
            P(),
            P(),
            P(),
            P(),
            P(),
            P("exp", None, "rep"),
            P("exp", "rep", None),
        ),
        check_vma=False,
    )
```

profile of v0, /device:TPU:0, one launch (start us, length us, event | category | flops | bytes accessed | tf_op | source)
XLA Modules:
  0.0 644.6 jit_solution(15393396317980434564)
XLA Ops:
  14.1 2.6 convolution_convert_fusion.1
  16.8 4.7 reshape.419
  21.5 4.9 fusion.134
  28.3 2.2 copy.223
  36.5 3.4 fusion.51
  43.5 13.5 %multiply_convert_fusion.2 = (bf16[788,1536]{1,0:T(8,128)(2,1)S(1)}, f32[788,1536]{1,0:T(8,128)}, f32[788,1536]{1,0:T(8,128)}) fusion(bf16[384,1536]{1,0:T(8,128)(2,1)S(1)} %copy-done, f32[788,384]{1,0:T(8,128)S(1)} %get-tuple-element.50, f32[384]{0:T(512)S(1)} %get-tuple-element.21, f32[788]{0:T(1024)S(1)} %fusion.116, f32[788]{0:T(1024)S(1)} %broadcast_multiply_fusion.3), kind=kOutput, calls=%fused_computation.48 | convolution fusion | flops 1009446912 | bytes 14501536 | tf_op jit(solution)/shard_map/dot_general | solution.py:118
  60.9 4.8 reshape.420
  65.7 4.9 fusion.133
  72.5 2.2 copy.226
  77.9 2.1 copy.224
  80.0 3.7 fusion.52
  85.2 2.0 convert_element_type.182
  87.3 2.4 fusion.137
  91.0 2.3 reduce-window.6
  97.1 3.0 reshape.403
  100.2 12.2 %scatter_custom_fusion = bf16[3152,384]{1,0:T(8,128)(2,1)} fusion(s32[1576]{0:T(1024)S(1)} %fusion.112, bf16[1576,384]{1,0:T(8,128)(2,1)S(1)} %reshape.403, bf16[]{:T(256)} %constant.75.clone.1), kind=kCustom, calls=%fused_computation.143 | custom fusion | bytes 2420738 | tf_op jit(solution)/shard_map/scatter | solution.py:170
  112.4 3.0 reshape.370
  115.4 4.1 copy.174
  119.5 5.5 all-to-all-start
  127.0 2.0 mul.475
  129.0 4.1 mul.482
  133.2 18.7 %scatter_custom_fusion.1 = bf16[3152,384]{1,0:T(8,128)(2,1)} fusion(s32[1576]{0:T(1024)S(1)} %fusion.112, f32[1576,384]{1,0:T(8,128)} %mul.482, f32[1576]{0:T(1024)S(1)} %div.109, bf16[]{:T(256)} %constant.75.clone.1), kind=kCustom, calls=%fused_computation.140 | custom fusion | flops 1210368 | bytes 4849666 | tf_op jit(solution)/shard_map/scatter | solution.py:199
  151.9 3.0 reshape.372
  154.9 4.2 copy.181
  159.2 4.9 all-to-all-start.2
  164.4 49.2 %fusion.9 = (bf16[2,4,394,1536]{3,2,0,1:T(8,128)(2,1)}, f32[2,4,394,1536]{3,2,0,1:T(8,128)}, f32[4,2,394,1536]{3,2,1,0:T(8,128)}) fusion(bf16[4,384,1536]{2,1,0:T(8,128)(2,1)} %param.19, bf16[2,4,394,384]{3,1,2,0:T(4,128)(2,1)} %all-to-all-done), kind=kOutput, calls=%fused_computation.21 | convolution fusion | flops 4032946176 | bytes 55554048 | tf_op jit(solution)/shard_map/sicd,idf->sicf/dot_general | solution.py:174
  213.6 11.2 %bitcast_convert_fusion = bf16[4,1536,384]{2,1,0:T(8,128)(2,1)} fusion(bf16[2,4,394,1536]{3,2,0,1:T(8,128)(2,1)} %get-tuple-element.36, bf16[2,4,394,384]{3,1,2,0:T(4,128)(2,1)} %all-to-all-done.2), kind=kOutput, calls=%fused_computation.35 | convolution fusion | flops 3720609792 | bytes 16822272 | tf_op jit(solution)/shard_map/sicf,sicd->ifd/dot_general | solution.py:203
  225.0 9.3 %convert_bitcast_fusion.1 = bf16[2,4,394,384]{3,2,0,1:T(8,128)(2,1)S(1)} fusion(bf16[2,4,394,1536]{3,2,0,1:T(8,128)(2,1)} %get-tuple-element.36, bf16[4,1536,384]{2,1,0:T(8,128)(2,1)} %param.20), kind=kOutput, calls=%fused_computation.81 | convolution fusion | flops 3719460864 | bytes 16822272 | tf_op jit(solution)/shard_map/sicf,ifd->sicd/dot_general | solution.py:178
  234.3 2.7 copy.176
  236.9 5.4 all-to-all-start.1
  242.4 24.3 %fusion.6 = bf16[2,4,394,1536]{3,2,0,1:T(8,128)(2,1)} fusion(f32[2,4,394,1536]{3,2,0,1:T(8,128)} %get-tuple-element.37, f32[4,2,394,1536]{3,2,1,0:T(8,128)} %get-tuple-element.58, bf16[4,1536,384]{2,1,0:T(8,128)(2,1)} %param.20, bf16[2,4,394,384]{3,1,2,0:T(4,128)(2,1)} %all-to-all-done.2), kind=kOutput, calls=%fused_computation.13 | convolution fusion | flops 3786031104 | bytes 55554048 | tf_op jit(solution)/shard_map/sicd,ifd->sicf/dot_general | solution.py:206
  266.6 9.3 %convert_bitcast_fusion = bf16[2,4,394,384]{3,2,0,1:T(8,128)(2,1)S(1)} fusion(bf16[2,4,394,1536]{3,2,0,1:T(8,128)(2,1)} %fusion.6, bf16[4,384,1536]{2,1,0:T(8,128)(2,1)} %param.19), kind=kOutput, calls=%fused_computation.80 | convolution fusion | flops 3719460864 | bytes 16822272 | tf_op jit(solution)/shard_map/sicf,idf->sicd/dot_general | solution.py:213
  276.0 2.8 copy.183
  278.7 5.0 all-to-all-start.3
  283.8 11.3 %bitcast_convert_fusion.1 = bf16[4,384,1536]{1,2,0:T(8,128)(2,1)} fusion(bf16[2,4,394,1536]{3,2,0,1:T(8,128)(2,1)} %fusion.6, bf16[2,4,394,384]{3,1,2,0:T(4,128)(2,1)} %all-to-all-done), kind=kOutput, calls=%fused_computation.36 | convolution fusion | flops 3720609792 | bytes 16822272 | tf_op jit(solution)/shard_map/sicd,sicf->idf/dot_general | solution.py:210
  295.3 3.4 copy.177
  298.7 3.1 reshape.371
  301.8 7.6 %gather_fusion = bf16[1576,384]{1,0:T(8,128)(2,1)} fusion(bf16[3152,384]{1,0:T(8,128)(2,1)} %reshape.371, s32[2048]{0:T(1024)S(1)} %pad_clamp_fusion), kind=kCustom, calls=%fused_computation | custom fusion | bytes 2427040 | tf_op jit(solution)/shard_map/gather | solution.py:182
  309.4 3.9 reshape.381
  313.3 10.7 %multiply_reduce_fusion.4 = (f32[788,2]{1,0:T(8,128)}, f32[788,384]{1,0:T(8,128)}) fusion(f32[788,2,384]{2,1,0:T(2,128)} %reshape.381, f32[788,384]{1,0:T(8,128)S(1)} %convert_element_type.191, f32[788,2]{1,0:T(8,128)S(1)} %copy-done.46), kind=kLoop, calls=%fused_computation.83 | loop fusion | flops 2116568 | bytes 4854080 | tf_op jit(solution)/shard_map/reduce_sum | solution.py:189
  325.4 3.6 copy.184
  329.0 3.1 reshape.373
  332.0 7.2 %gather_fusion.1 = bf16[1576,384]{1,0:T(8,128)(2,1)S(1)} fusion(bf16[3152,384]{1,0:T(8,128)(2,1)} %reshape.373, s32[2048]{0:T(1024)S(1)} %pad_clamp_fusion), kind=kCustom, calls=%fused_computation.1 | custom fusion | bytes 2427040 | tf_op jit(solution)/shard_map/gather | solution.py:217
  339.2 2.6 reshape.382
  341.9 5.7 reduce_sum.315
  347.6 2.1 multiply_reduce_fusion.6
  354.8 2.4 copy.186
  357.2 4.0 multiply_reduce_fusion.1
  366.0 3.4 copy.191
  369.4 5.5 convert_element_type.203
  374.9 3.5 multiply_reduce_fusion.7
  380.5 5.7 add_convert_fusion
  392.4 2.7 copy.193
  395.1 4.4 multiply_reduce_fusion
  404.5 3.4 copy.198
  407.9 5.7 convert_element_type.210
  421.4 3.2 fusion.94
  424.6 2.0 pad_maximum_fusion
  427.9 3.0 fusion.126
  431.0 3.4 fusion.56
  436.3 44.7 %all-reduce.1 = (f32[4,384]{1,0:T(4,128)}, f32[384,8]{0,1:T(8,128)}) all-reduce(f32[4,384]{1,0:T(4,128)S(1)} %pad_maximum_fusion.2, f32[384,8]{0,1:T(8,128)S(1)} %fusion.139), channel_id=1, replica_groups=mesh['rep'=16,'exp'=2] {'rep','exp'}, use_global_device_ids=true, to_apply=%region_41.42 | all-reduce | flops 4608 | bytes 36864 | tf_op jit(solution)/shard_map/psum | solution.py:242
  481.0 2.8 add_add_fusion.4
  487.4 139.4 %all-reduce.5.cloned.1.call-done = (f32[2,384,1152]{2,1,0:T(8,128)}, f32[2,384,384]{2,1,0:T(8,128)}, f32[384,1536]{1,0:T(8,128)}, f32[1536,384]{1,0:T(8,128)}) async-done(((f32[2,384,1152]{2,1,0:T(8,128)}, f32[2,384,384]{2,1,0:T(8,128)}, f32[384,1536]{1,0:T(8,128)}, f32[1536,384]{1,0:T(8,128)}), (f32[2,384,1152]{2,1,0:T(8,128)}, f32[2,384,384]{2,1,0:T(8,128)}, f32[384,1536]{1,0:T(8,128)}, ...) | async-done | bytes 9437200 | tf_op jit(solution)/shard_map/psum | solution.py:242
  626.8 4.1 copy.244
  (341 shorter events, 80.0 us)
Async XLA Ops:
  8.0 35.5 %copy-start = (bf16[384,1536]{1,0:T(8,128)(2,1)S(1)}, bf16[384,1536]{1,0:T(8,128)(2,1)}, u32[]{:S(2)}) copy-start(bf16[384,1536]{1,0:T(8,128)(2,1)} %param.16) | copy-start | bytes 3538948
  13.2 8.3 %copy-start.89 = (f32[788]{0:T(1024)}, f32[788]{0:T(1024)S(1)}, u32[]{:S(2)}) copy-start(f32[788]{0:T(1024)S(1)} %fusion.115) | copy-start | bytes 9460
  14.1 7.4 %copy-start.97 = (f32[384]{0:T(512)}, f32[384]{0:T(512)S(1)}, u32[]{:S(2)}) copy-start(f32[384]{0:T(512)S(1)} %get-tuple-element.22) | copy-start | bytes 4612
  14.1 29.4 %copy-start.79 = (f32[384]{0:T(512)}, f32[384]{0:T(512)S(1)}, u32[]{:S(2)}) copy-start(f32[384]{0:T(512)S(1)} %get-tuple-element.21) | copy-start | bytes 4612
  14.1 45.5 %copy-start.101 = (f32[384]{0:T(512)}, f32[384]{0:T(512)S(1)}, u32[]{:S(2)}) copy-start(f32[384]{0:T(512)S(1)} %get-tuple-element.23) | copy-start | bytes 4612
  14.1 80.2 %copy-start.93 = (f32[384]{0:T(512)}, f32[384]{0:T(512)S(1)}, u32[]{:S(2)}) copy-start(f32[384]{0:T(512)S(1)} %get-tuple-element.20) | copy-start | bytes 4612
  33.6 6.3 copy-start.57
  41.1 15.9 %copy-start.37 = (bf16[788,384]{0,1:T(8,128)(2,1)}, bf16[788,384]{0,1:T(8,128)(2,1)S(1)}, u32[]{:S(2)}) copy-start(bf16[788,384]{0,1:T(8,128)(2,1)S(1)} %convert_element_type.174) | copy-start | bytes 1815556
  43.1 14.0 %copy-start.7 = (f32[788,384]{1,0:T(8,128)}, f32[788,384]{1,0:T(8,128)S(1)}, u32[]{:S(2)}) copy-start(f32[788,384]{1,0:T(8,128)S(1)} %get-tuple-element.50) | copy-start | bytes 3631108
  43.1 13.9 %copy-start.63 = (f32[788]{0:T(1024)}, f32[788]{0:T(1024)S(1)}, u32[]{:S(2)}) copy-start(f32[788]{0:T(1024)S(1)} %broadcast_multiply_fusion.3) | copy-start | bytes 9460
  43.4 13.6 %copy-start.83 = (f32[788]{0:T(1024)}, f32[788]{0:T(1024)S(1)}, u32[]{:S(2)}) copy-start(f32[788]{0:T(1024)S(1)} %multiply_reduce_fusion.14) | copy-start | bytes 9460
  43.4 13.6 %copy-start.71 = (f32[788]{0:T(1024)}, f32[788]{0:T(1024)S(1)}, u32[]{:S(2)}) copy-start(f32[788]{0:T(1024)S(1)} %fusion.116) | copy-start | bytes 9460
  43.5 13.6 %copy-start.104 = (bf16[1536,384]{1,0:T(8,128)(2,1)S(1)}, bf16[1536,384]{1,0:T(8,128)(2,1)}, u32[]{:S(2)}) copy-start(bf16[1536,384]{1,0:T(8,128)(2,1)} %param.17) | copy-start | bytes 3538948
  59.6 6.1 copy-start.99
  77.9 5.9 copy-start.59
  80.0 3.7 copy-start.26
  87.3 3.6 copy-start.39
  89.7 5.0 copy-start.3
  89.7 4.9 copy-start.67
  90.7 6.5 %copy-start.73 = (f32[788]{0:T(1024)}, f32[788]{0:T(1024)S(1)}, u32[]{:S(2)}) copy-start(f32[788]{0:T(1024)S(1)} %fusion.118) | copy-start | bytes 9460
  119.5 5.5 copy-start.23
  119.5 5.5 copy-start.95
  119.5 5.8 copy-start.65
  119.5 7.5 %copy-start.15 = (bf16[788,384]{1,0:T(8,128)(2,1)S(1)}, bf16[788,384]{1,0:T(8,128)(2,1)}, u32[]{:S(2)}) copy-start(bf16[788,384]{1,0:T(8,128)(2,1)} %param.21) | copy-start | bytes 1815556
  119.5 39.7 %all-to-all-start = ((bf16[2,4,394,384]{3,1,2,0:T(4,128)(2,1)}), bf16[2,4,394,384]{3,1,2,0:T(4,128)(2,1)}, u32[]{:S(2)}, u32[]{:S(2)}) async-start(bf16[2,4,394,384]{3,1,2,0:T(4,128)(2,1)} %copy.174), calls=%async_computation | async-start | bytes 4841472 | tf_op jit(solution)/shard_map/all_to_all | solution.py:173
  126.7 6.4 copy-start.45
  159.2 54.4 %all-to-all-start.2 = ((bf16[2,4,394,384]{3,1,2,0:T(4,128)(2,1)}), bf16[2,4,394,384]{3,1,2,0:T(4,128)(2,1)}, u32[]{:S(2)}, u32[]{:S(2)}) async-start(bf16[2,4,394,384]{3,1,2,0:T(4,128)(2,1)} %copy.181), calls=%async_computation.2 | async-start | bytes 4841472 | tf_op jit(solution)/shard_map/all_to_all | solution.py:202
  164.1 319.6 %reduce-scatter.5.cloned.1.call-start = ((), (), s32[]{:S(2)}) async-start(), calls=%async_computation.7 | async-start | bytes 5013504 | tf_op jit(solution)/shard_map/reduce_scatter | solution.py:238
  236.9 41.8 %all-to-all-start.1 = ((bf16[2,4,394,384]{3,1,2,0:T(4,128)(2,1)}), bf16[2,4,394,384]{3,1,2,0:T(4,128)(2,1)}, u32[]{:S(2)}, u32[]{:S(2)}) async-start(bf16[2,4,394,384]{3,1,2,0:T(4,128)(2,1)} %copy.176), calls=%async_computation.1 | async-start | bytes 4841472 | tf_op jit(solution)/shard_map/all_to_all | solution.py:181
  278.7 46.7 %all-to-all-start.3 = ((bf16[2,4,394,384]{3,1,2,0:T(4,128)(2,1)}), bf16[2,4,394,384]{3,1,2,0:T(4,128)(2,1)}, u32[]{:S(2)}, u32[]{:S(2)}) async-start(bf16[2,4,394,384]{3,1,2,0:T(4,128)(2,1)} %copy.183), calls=%async_computation.3 | async-start | bytes 4841472 | tf_op jit(solution)/shard_map/all_to_all | solution.py:216
  283.7 201.9 %reduce-scatter.3.cloned.1.call-start = ((), (), s32[]{:S(2)}) async-start(), calls=%async_computation.6 | async-start | bytes 5013504 | tf_op jit(solution)/shard_map/reduce_scatter | solution.py:235
  295.0 331.8 %all-reduce.5.cloned.1.call-start = ((), (), s32[]{:S(2)}) async-start(), calls=%async_computation.8 | async-start | bytes 18874368 | tf_op jit(solution)/shard_map/psum | solution.py:242
  309.4 3.9 copy-start.46
  313.3 12.0 %copy-start.62 = (f32[788,2]{0,1:T(2,128)S(1)}, f32[788,2]{0,1:T(2,128)}, u32[]{:S(2)}) copy-start(f32[788,2]{0,1:T(2,128)} %copy-done.61) | copy-start | bytes 18916
  313.3 12.0 %copy-start.70 = (f32[788]{0:T(1024)S(1)}, f32[788]{0:T(1024)}, u32[]{:S(2)}) copy-start(f32[788]{0:T(1024)} %copy-done.69) | copy-start | bytes 9460
  313.3 12.0 %copy-start.76 = (f32[788]{0:T(1024)S(1)}, f32[788]{0:T(1024)}, u32[]{:S(2)}) copy-start(f32[788]{0:T(1024)} %copy-done.75) | copy-start | bytes 9460
  313.3 12.0 %copy-start.66 = (s32[788,2]{0,1:T(2,128)S(1)}, s32[788,2]{0,1:T(2,128)}, u32[]{:S(2)}) copy-start(s32[788,2]{0,1:T(2,128)} %param.12) | copy-start | bytes 18916
  341.8 5.7 copy-start.4
  341.8 5.7 copy-start.68
  341.8 5.7 copy-start.74
  341.9 5.7 copy-start.94
  341.9 5.7 copy-start.96
  352.7 4.4 copy-start.27
  352.7 4.4 copy-start.60
  354.8 6.4 slice-start.2
  357.2 4.0 slice-start.3
  369.4 5.5 copy-start.19
  369.4 5.5 copy-start.92
  369.4 5.5 copy-start.100
  369.4 5.5 copy-start.102
  374.9 3.6 copy-start.20
  380.3 8.2 %copy-start.41 = (f32[788,384]{1,0:T(8,128)}, f32[788,384]{1,0:T(8,128)S(1)}, u32[]{:S(2)}) copy-start(f32[788,384]{1,0:T(8,128)S(1)} %add_add_fusion.6) | copy-start | bytes 3631108
  380.5 5.7 copy-start.8
  380.5 5.7 copy-start.64
  380.5 5.7 copy-start.72
  380.5 5.7 copy-start.80
  390.3 4.7 copy-start.58
  392.4 7.1 %slice-start = ((s8[4915200]{0:T(1024)(128)(4,1)}), s8[720896]{0:T(1024)(128)(4,1)S(1)}, s32[]{:S(2)}) async-start(s8[4915200]{0:T(1024)(128)(4,1)} %bitcast.269), calls=%async_computation.9 | async-start | bytes 1441792
  395.1 4.4 slice-start.1
  407.9 5.7 copy-start.38
  430.9 4.4 copy-start.14
  431.0 5.1 copy-start.24
  434.3 46.6 %copy-start.11 = (f32[788,384]{1,0:T(8,128)S(1)}, f32[788,384]{1,0:T(8,128)}, u32[]{:S(2)}) copy-start(f32[788,384]{1,0:T(8,128)} %copy-done.10) | copy-start | bytes 3631108
  626.8 4.1 copy-start.56
  (55 other events, 92.7 us)
Sparse Core Ops, SparseCore 0:
  225.0 78.7 reduce-scatter.4
  307.6 74.5 reduce-scatter.2
Sparse Core Ops, SparseCore 1:
  431.0 195.8 all-reduce.4
where the time goes:
time: 655 us; the launch traced here: 645 us
  matrix products  190 us (29%)
  local copies, waits for them, and re-layouts  171 us (26%)
  waiting for transfers between devices  139 us (21%)
  other arithmetic  61.1 us (9%)
  blocking collectives  44.7 us (7%)
  starting transfers between devices  21.3 us (3%)
  between operations  17.4 us (3%)
    psum x1, waiting for transfers between devices, shards(): lax.psum((jnp.stack([grad_qkv_one, grad_qkv_two]), jnp.stack([grad_proj_o...  139 us
    dot_general x1, matrix products, shards(): jnp.einsum('sicd,idf->sicf', incoming, experts_in, preferred_element_type...  49.2 us
    psum x1, blocking collectives, shards(): lax.psum((jnp.stack([grad_qkv_one, grad_qkv_two]), jnp.stack([grad_proj_o...  44.7 us
    unnamed x236, local copies, waits for them, and re-layouts  38.7 us
    dot_general x1, matrix products, shards(): jnp.einsum('sicd,ifd->sicf', incoming_grad, experts_out, preferred_elemen...  24.3 us
    scatter x1, other arithmetic, shards(): outgoing_grad = jnp.zeros((experts * capacity, model_width), jnp.bfloat16...  18.7 us
    convert_element_type x4, local copies, waits for them, and re-layouts, attend_backward(): grad_qkv = jnp.stack([grad_query, grad_key, grad_value], axis=2).reshape(...  18 us
    dot_general x1, matrix products, dense_forward(): hidden = jnp.dot(normed, w_in, preferred_element_type=jnp.float32)  13.5 us
  transfers between devices with their start and end apart: 7, of which 1 were waited for; matrix products, arithmetic and copies ran while one was open for 44% of the time, Pallas kernels for 0%

commit v1 on v0

v1 whole, which is shorter than its diff:
```python
import functools

import jax
import jax.numpy as jnp
from jax import lax
from jax.experimental import pallas as pl
from jax.experimental.pallas import tpu as pltpu
from jax.sharding import PartitionSpec as P

F32 = jnp.float32
BF = jnp.bfloat16
HEADS = 6
PATCHES = 197
ROWS = 208
EPS = 1e-6
TILE = 128
CHUNK = 1024
D = 384
FF = 1536
VMEM = pl.BlockSpec(memory_space=pltpu.VMEM)


def dot(a, b):
    return lax.dot_general(a, b, (((1,), (0,)), ((), ())), preferred_element_type=F32)


def dot_t(a, b):
    return lax.dot_general(a, b, (((1,), (1,)), ((), ())), preferred_element_type=F32)


def t_dot(a, b):
    return lax.dot_general(a, b, (((0,), (0,)), ((), ())), preferred_element_type=F32)


def norm_parts(x):
    centred = x - jnp.mean(x, axis=-1, keepdims=True)
    rstd = lax.rsqrt(jnp.mean(centred * centred, axis=-1, keepdims=True) + EPS)
    return centred * rstd, rstd


def norm_back(grad, x, gain):
    xh, rstd = norm_parts(x)
    dxh = grad * gain
    inner = dxh - jnp.mean(dxh, axis=-1, keepdims=True)
    return rstd * (inner - xh * jnp.mean(dxh * xh, axis=-1, keepdims=True)), grad * xh


def gelu_parts(h):
    t = 1.0 / (1.0 + (0.3275911 * 0.7071067811865476) * jnp.abs(h))
    e = jnp.exp(-0.5 * h * h)
    poly = t * (
        0.254829592
        + t * (-0.284496736 + t * (1.421413741 + t * (-1.453152027 + t * 1.061405429)))
    )
    tail = 0.5 * poly * e
    phi = jnp.where(h >= 0, 1.0 - tail, tail)
    return h * phi, phi + h * (0.3989422804014327 * e)


def lane_low(rows):
    return lax.broadcasted_iota(jnp.int32, (rows, 128), 1) < 64


def fwd_kernel(
    x_ref, gains, wqkv, wo, win, wout,
    x1_ref, x2_ref, x3_ref, qkv1_ref, qkv2_ref, o1_ref, o2_ref, p1_ref, p2_ref, u_ref, gp_ref, c_ref,
):
    ib = x_ref.shape[0]
    m = ib * ROWS
    lo = lane_low(ROWS)
    valid = lax.broadcasted_iota(jnp.int32, (ROWS, ROWS), 1) < PATCHES

    def attend(x, layer, gain, qkv_ref, o_ref, p_ref):
        a = (norm_parts(x)[0] * gain).astype(BF)
        qkv_ref[...] = dot(a, wqkv[layer]).astype(BF).reshape(ib, ROWS, 3 * D)
        for i in range(ib):
            for pair in range(HEADS // 2):
                at = 128 * pair
                q = qkv_ref[i, :, at : at + 128] * BF(0.125)
                k = qkv_ref[i, :, D + at : D + at + 128]
                w = qkv_ref[i, :, 2 * D + at : 2 * D + at + 128]
                mixed = []
                for h in range(2):
                    qm = jnp.where(lo if h == 0 else ~lo, q, BF(0))
                    s = jnp.where(valid, dot_t(qm, k), -1e30)
                    s = jnp.exp(s - jnp.max(s, axis=-1, keepdims=True))
                    p = (s * (1.0 / jnp.sum(s, axis=-1, keepdims=True))).astype(BF)
                    p_ref[i, 2 * pair + h] = p
                    mixed.append(dot(p, w))
                o_ref[i, :, at : at + 128] = jnp.where(lo, mixed[0], mixed[1]).astype(BF)
        return x + dot(o_ref[...].reshape(m, D), wo[layer])

    x0 = x_ref[...].astype(F32).reshape(m, D)
    x1 = attend(x0, 0, gains[0:1], qkv1_ref, o1_ref, p1_ref)
    x1_ref[...] = x1.reshape(ib, ROWS, D)
    b = (norm_parts(x1)[0] * gains[1:2]).astype(BF)
    x2 = x1
    for f in range(0, FF, 512):
        u, gp = gelu_parts(dot(b, win[:, f : f + 512]))
        u = u.astype(BF)
        u_ref[:, :, f : f + 512] = u.reshape(ib, ROWS, 512)
        gp_ref[:, :, f : f + 512] = gp.astype(BF).reshape(ib, ROWS, 512)
        x2 = x2 + dot(u, wout[f : f + 512])
    x2_ref[...] = x2.reshape(ib, ROWS, D)
    x3 = attend(x2, 1, gains[2:3], qkv2_ref, o2_ref, p2_ref)
    x3_ref[...] = x3.reshape(ib, ROWS, D)
    c_ref[...] = (norm_parts(x3)[0] * gains[3:4]).astype(BF).reshape(ib, ROWS, D)


def dense_forward(x, gains, wqkv, wo, win, wout):
    n = x.shape[0]
    ib = 2 if n % 2 == 0 else 1

    def out(*shape, dtype=BF):
        return jax.ShapeDtypeStruct((n,) + shape, dtype)

    def block(shape):
        return pl.BlockSpec((ib,) + tuple(shape[1:]), lambda i: (i,) + (0,) * (len(shape) - 1))

    outs = [out(ROWS, D, dtype=F32)] * 3 + [out(ROWS, 3 * D)] * 2 + [out(ROWS, D)] * 2
    outs += [out(HEADS, ROWS, ROWS)] * 2 + [out(ROWS, FF)] * 2 + [out(ROWS, D)]
    return pl.pallas_call(
        fwd_kernel,
        grid=(n // ib,),
        out_shape=outs,
        in_specs=[block(x.shape)] + [VMEM] * 5,
        out_specs=[block(o.shape) for o in outs],
        compiler_params=pltpu.CompilerParams(vmem_limit_bytes=60 << 20),
        name="dense_forward",
    )(x, gains, wqkv, wo, win, wout)


def gate_rows(router_t, c, routes):
    logits = dot_t(router_t, c)
    expert = lax.broadcasted_iota(jnp.int32, logits.shape, 0)
    first, second = expert == routes[0:1], expert == routes[1:2]
    diff = jnp.sum(jnp.where(first, logits, 0.0) - jnp.where(second, logits, 0.0), axis=0, keepdims=True)
    return 1.0 / (1.0 + jnp.exp(-diff)), 1.0 / (1.0 + jnp.exp(diff)), first, second


def experts_kernel(groups, local, exp_axis, *refs):
    c_refs, g_refs, r_refs = refs[:groups], refs[groups : 2 * groups], refs[2 * groups : 3 * groups]
    router_t, win, wout = refs[3 * groups : 3 * groups + 3]
    outs = refs[3 * groups + 3 :]
    eg_ref, y_refs, d_refs, delta_refs = outs[0], outs[1 : groups + 1], outs[groups + 1 : 2 * groups + 1], outs[2 * groups + 1 : 3 * groups + 1]
    ci, g4, rows, cols, slots, acc_out, acc_in, u_scr, gp_scr, back, counts = outs[3 * groups + 1 :]
    n_tok = c_refs[0].shape[0]
    total = groups * n_tok
    step = pl.program_id(0)
    first_expert = lax.axis_index(exp_axis) * local

    @pl.when(step == 0)
    def _():
        for s in range(groups):
            at = s * n_tok
            ci[at : at + n_tok, 0:D] = c_refs[s][...]
            g4[at : at + n_tok] = g_refs[s][...]
        routes = jnp.concatenate([r[0:2] for r in r_refs], axis=1)
        g0, g1, _, _ = gate_rows(router_t[...], ci[:, 0:D], routes)
        mine = first_expert + lax.broadcasted_iota(jnp.int32, (8, total), 0)
        inside = lax.broadcasted_iota(jnp.int32, (8, total), 0) < local
        is0, is1 = (mine == routes[0:1]) & inside, (mine == routes[1:2]) & inside
        member = jnp.where(is0 | is1, 1.0, 0.0)
        lane = lax.broadcasted_iota(jnp.int32, (8, total), 1)
        upto = member
        shift = 1
        while shift < total:
            upto = upto + jnp.where(lane >= shift, pltpu.roll(upto, shift, 1), 0.0)
            shift *= 2
        position = jnp.where(member > 0, upto - 1.0, -1.0)
        rows[0:8] = position
        base = jnp.int32(0)
        starts = []
        for e in range(local):
            n = jnp.sum(member[e : e + 1]).astype(jnp.int32)
            tiles = (n + TILE - 1) // TILE
            counts[e] = tiles
            counts[8 + e] = base
            starts.append((base * TILE).astype(F32))
            base = base + tiles
        counts[16] = base
        start = jnp.zeros((8, total), F32)
        expert_row = lax.broadcasted_iota(jnp.int32, (8, total), 0)
        for e in range(local):
            start = jnp.where(expert_row == e, starts[e], start)
        slot = start + position
        slot0 = jnp.sum(jnp.where(is0, slot + 1.0, 0.0), axis=0, keepdims=True) - 1.0
        slot1 = jnp.sum(jnp.where(is1, slot + 1.0, 0.0), axis=0, keepdims=True) - 1.0
        gates = jnp.where(is0, g0, jnp.where(is1, g1, 0.0))
        sign = jnp.where(is0, 1.0, jnp.where(is1, -1.0, 0.0))
        slot_rows = jnp.where(expert_row == 0, slot0, jnp.where(expert_row == 1, slot1, 0.0))
        stacked = jnp.concatenate([gates, sign, slot_rows, jnp.zeros((104, total), F32)], axis=0)
        lane128 = lax.broadcasted_iota(jnp.int32, (128, 128), 1)
        for at in range(0, total, 128):
            col = stacked[:, at : at + 128].T
            cols[at : at + 128] = col
            low = col - col.astype(BF).astype(F32)
            info = jnp.where(lane128 < 16, col, jnp.where(lane128 < 24, pltpu.roll(low, 16, 1), 0.0))
            ci[at : at + 128, D : D + 128] = info.astype(BF)

    acc_out[...] = jnp.zeros_like(acc_out)
    acc_in[...] = jnp.zeros_like(acc_in)
    position = rows[pl.ds(step, 1)]
    lane = lax.broadcasted_iota(jnp.int32, (TILE, 128), 1)

    def tile(j, _):
        slot = (j * TILE + lax.broadcasted_iota(jnp.int32, (TILE, total), 0)).astype(F32)
        pick = jnp.where(position == slot, 1.0, 0.0).astype(BF)
        xi = dot(pick, ci[...])
        g4r = dot(pick, g4[...])
        x = xi[:, 0:D].astype(BF)
        info = xi[:, D : D + 128]
        gate = jnp.sum(jnp.where((lane == step) | (lane == step + 16), info, 0.0), axis=-1, keepdims=True)
        sign = jnp.sum(jnp.where(lane == step + 8, info, 0.0), axis=-1, keepdims=True)
        dy = (gate * g4r).astype(BF)
        for f in range(0, FF, 512):
            u, gp = gelu_parts(dot(x, win[0, :, f : f + 512]))
            u_scr[:, f : f + 512] = u.astype(BF)
            gp_scr[:, f : f + 512] = gp.astype(BF)
        ey = dot(u_scr[...], wout[0]).astype(BF).astype(F32)
        dg = sign * jnp.sum(g4r * ey, axis=-1, keepdims=True)
        acc_out[...] += t_dot(u_scr[...], dy)
        for f in range(0, FF, 512):
            du = dot_t(dy, wout[0, f : f + 512])
            gp_scr[:, f : f + 512] = (du * gp_scr[:, f : f + 512].astype(F32)).astype(BF)
        dcp = dot_t(gp_scr[...], win[0])
        acc_in[...] += t_dot(gp_scr[...], x)
        at = pl.multiple_of((counts[8 + step] + j) * TILE, TILE)
        slots[pl.ds(at, TILE), 0:D] = (gate * ey).astype(BF)
        slots[pl.ds(at, TILE), D : 2 * D] = dcp.astype(BF)
        low = dg - dg.astype(BF).astype(F32)
        slots[pl.ds(at, TILE), 2 * D : 2 * D + 128] = jnp.where(lane == 0, dg, jnp.where(lane == 1, low, 0.0)).astype(BF)
        return 0

    lax.fori_loop(0, counts[step], tile, 0)
    eg_ref[0, 0] = acc_in[...].astype(BF)
    eg_ref[0, 1] = acc_out[...].astype(BF)

    @pl.when(step == local - 1)
    def _():
        used = counts[16]
        chunks = (used * TILE + CHUNK - 1) // CHUNK

        def clear(j, _):
            at = pl.multiple_of(j * TILE, TILE)
            slots[pl.ds(at, TILE)] = jnp.zeros((TILE, 2 * D + 128), BF)
            return 0

        lax.fori_loop(used, chunks * (CHUNK // TILE), clear, 0)
        lane_chunk = lax.broadcasted_iota(jnp.int32, (ROWS, CHUNK), 1)

        for s in range(groups):
            for b in range(n_tok // ROWS):
                at = s * n_tok + b * ROWS
                slot0, slot1 = cols[at : at + ROWS, 16:17], cols[at : at + ROWS, 17:18]
                back[...] = jnp.zeros_like(back)

                def gather(j, _):
                    slot = (j * CHUNK + lane_chunk).astype(F32)
                    pick = jnp.where((slot0 == slot) | (slot1 == slot), 1.0, 0.0).astype(BF)
                    back[...] += dot(pick, slots[pl.ds(pl.multiple_of(j * CHUNK, CHUNK), CHUNK)])
                    return 0

                lax.fori_loop(0, chunks, gather, 0)
                y_refs[s][b * ROWS : (b + 1) * ROWS] = back[:, 0:D].astype(BF)
                d_refs[s][b * ROWS : (b + 1) * ROWS] = back[:, D : 2 * D].astype(BF)
                cols[at : at + ROWS] = back[:, 2 * D : 2 * D + 128]
        for at in range(0, total, 128):
            rows[:, at : at + 128] = cols[at : at + 128].T[0:8]
        for s in range(groups):
            delta_refs[s][...] = rows[:, s * n_tok : (s + 1) * n_tok]


def experts_all(cs, gs, rs, router_t, win, wout, slots_most):
    groups = len(cs)
    local = win.shape[0]
    n_tok = cs[0].shape[0]
    total = groups * n_tok
    room = -(-(slots_most + local * TILE) // CHUNK) * CHUNK

    def full(shape):
        return pl.BlockSpec(tuple(shape), lambda i: (0,) * len(shape))

    outs = [jax.ShapeDtypeStruct((local, 2, FF, D), BF)]
    outs += [jax.ShapeDtypeStruct((n_tok, D), BF)] * (2 * groups)
    outs += [jax.ShapeDtypeStruct((8, n_tok), F32)] * groups
    result = pl.pallas_call(
        functools.partial(experts_kernel, groups, local, "exp"),
        grid=(local,),
        out_shape=outs,
        in_specs=[VMEM] * (3 * groups + 1)
        + [pl.BlockSpec((1, D, FF), lambda i: (i, 0, 0)), pl.BlockSpec((1, FF, D), lambda i: (i, 0, 0))],
        out_specs=[pl.BlockSpec((1, 2, FF, D), lambda i: (i, 0, 0, 0))] + [full(o.shape) for o in outs[1:]],
        scratch_shapes=[
            pltpu.VMEM((total, D + 128), BF),
            pltpu.VMEM((total, D), BF),
            pltpu.VMEM((8, total), F32),
            pltpu.VMEM((total, 128), F32),
            pltpu.VMEM((room, 2 * D + 128), BF),
            pltpu.VMEM((FF, D), F32),
            pltpu.VMEM((FF, D), F32),
            pltpu.VMEM((TILE, FF), BF),
            pltpu.VMEM((TILE, FF), BF),
            pltpu.VMEM((ROWS, 2 * D + 128), F32),
            pltpu.SMEM((24,), jnp.int32),
        ],
        compiler_params=pltpu.CompilerParams(vmem_limit_bytes=60 << 20),
        name="experts",
    )(*cs, *gs, *rs, router_t, win, wout)
    return result[0], result[1 : groups + 1], result[groups + 1 : 2 * groups + 1], result[2 * groups + 1 :]


def bwd_kernel(groups, n_in, *refs):
    ins, outs, scr = refs[:n_in], refs[n_in : n_in + 10], refs[n_in + 10 :]
    (gains, wqkv, wo, win, wout, router_t, x0, x1, x2, x3, qkv1, qkv2, o1, o2, p1, p2, u, gp, c, cot, routes) = ins[:21]
    y_refs, d_refs, delta_refs = ins[21 : 21 + groups], ins[21 + groups : 21 + 2 * groups], ins[21 + 2 * groups :]
    act, gin, dqkv_a, dqkv_b, dproj_a, dproj_b, dgain, dwin, dwout, drouter = outs
    gv, a_scr, dbr_scr, big = scr
    images = x0.shape[0]
    m = images * ROWS
    lo = lane_low(ROWS)

    g0, g1, first, second = gate_rows(router_t[...], c[...].reshape(m, D), routes[...])
    delta = delta_refs[0][0:1] + delta_refs[0][1:2]
    for r in delta_refs[1:]:
        delta = delta + (r[0:1] + r[1:2])
    dl = g0 * g1 * delta
    dlog = jnp.where(first, dl, jnp.where(second, -dl, 0.0)).astype(BF)
    drouter[...] = dot(dlog, c[...].reshape(m, D))
    gv[...] = t_dot(dlog, router_t[...]).reshape(images, ROWS, D)

    def open_image(i, total):
        y = y_refs[0][i].astype(F32)
        dc = gv[i] + d_refs[0][i].astype(F32)
        for k in range(1, groups):
            y = y + y_refs[k][i].astype(F32)
            dc = dc + d_refs[k][i].astype(F32)
        act[i] = (x3[i] + y).astype(BF)
        dx, by_gain = norm_back(dc, x3[i], gains[3:4])
        gv[i] = cot[i].astype(F32) + dx
        return total + jnp.sum(by_gain, axis=0, keepdims=True)

    dgain[3:4] = lax.fori_loop(0, images, open_image, jnp.zeros((1, D), F32))

    def attend_back(layer, gain_row, x, qkv, o, p, dqkv_out, dproj_out, last):
        gain = gains[gain_row : gain_row + 1]

        def image(i, _):
            a_scr[i] = (norm_parts(x[i].astype(F32))[0] * gain).astype(BF)
            dbr = gv[i].astype(BF)
            dbr_scr[i] = dbr
            do = dot_t(dbr, wo[layer])
            dod = do.astype(BF).astype(F32) * o[i].astype(F32)
            do = do.astype(BF)
            for pair in range(HEADS // 2):
                at = 128 * pair
                q = qkv[i, :, at : at + 128] * BF(0.125)
                k = qkv[i, :, D + at : D + at + 128]
                w = qkv[i, :, 2 * D + at : 2 * D + at + 128]
                dqs, dk, dw = [], 0.0, 0.0
                for h in range(2):
                    mask = lo if h == 0 else ~lo
                    dom = jnp.where(mask, do[:, at : at + 128], BF(0))
                    inner = jnp.sum(jnp.where(mask, dod[:, at : at + 128], 0.0), axis=-1, keepdims=True)
                    ph = p[i, 2 * pair + h]
                    ds = (ph.astype(F32) * (dot_t(dom, w) - inner)).astype(BF)
                    dw = dw + t_dot(ph, dom)
                    dqs.append(dot(ds, k))
                    dk = dk + t_dot(ds, jnp.where(mask, q, BF(0)))
                big[i, :, at : at + 128] = (jnp.where(lo, dqs[0], dqs[1]) * 0.125).astype(BF)
                big[i, :, D + at : D + at + 128] = dk.astype(BF)
                big[i, :, 2 * D + at : 2 * D + at + 128] = dw.astype(BF)
            return 0

        lax.fori_loop(0, images, image, 0)
        dproj_out[...] = t_dot(o[...].reshape(m, D), dbr_scr[...].reshape(m, D)).astype(BF)
        a_all = a_scr[...].reshape(m, D)
        for f in range(0, 3 * D, D):
            dqkv_out[:, f : f + D] = t_dot(a_all, big[:, :, f : f + D].reshape(m, D)).astype(BF)

        def close(i, total):
            da = dot_t(big[i, :, 0 : 3 * D], wqkv[layer])
            dx, by_gain = norm_back(da, x[i].astype(F32), gain)
            new = gv[i] + dx
            if last:
                gin[i] = new
            else:
                gv[i] = new
            return total + jnp.sum(by_gain, axis=0, keepdims=True)

        dgain[gain_row : gain_row + 1] = lax.fori_loop(0, images, close, jnp.zeros((1, D), F32))

    attend_back(1, 2, x2, qkv2, o2, p2, dqkv_b, dproj_b, False)

    def mlp_image(i, _):
        a_scr[i] = (norm_parts(x1[i])[0] * gains[1:2]).astype(BF)
        dm = gv[i].astype(BF)
        dbr_scr[i] = dm
        for f in range(0, FF, 512):
            big[i, :, f : f + 512] = (dot_t(dm, wout[f : f + 512]) * gp[i, :, f : f + 512].astype(F32)).astype(BF)
        return 0

    lax.fori_loop(0, images, mlp_image, 0)
    dm_all = dbr_scr[...].reshape(m, D)
    b_all = a_scr[...].reshape(m, D)
    for f in range(0, FF, 512):
        dwout[f : f + 512] = t_dot(u[:, :, f : f + 512].reshape(m, 512), dm_all).astype(BF)
        dwin[:, f : f + 512] = t_dot(b_all, big[:, :, f : f + 512].reshape(m, 512)).astype(BF)

    def mlp_close(i, total):
        db = dot_t(big[i], win[...])
        dx, by_gain = norm_back(db, x1[i], gains[1:2])
        gv[i] = gv[i] + dx
        return total + jnp.sum(by_gain, axis=0, keepdims=True)

    dgain[1:2] = lax.fori_loop(0, images, mlp_close, jnp.zeros((1, D), F32))

    attend_back(0, 0, x0, qkv1, o1, p1, dqkv_a, dproj_a, True)


def dense_backward(weights, saved, cot, routes, ys, ds, deltas):
    groups = len(ys)
    images = saved[0].shape[0]
    experts = weights[-1].shape[0]
    ins = list(weights) + list(saved) + [cot, routes] + list(ys) + list(ds) + list(deltas)
    outs = [
        jax.ShapeDtypeStruct((images, ROWS, D), BF),
        jax.ShapeDtypeStruct((images, ROWS, D), F32),
        jax.ShapeDtypeStruct((D, 3 * D), BF),
        jax.ShapeDtypeStruct((D, 3 * D), BF),
        jax.ShapeDtypeStruct((D, D), BF),
        jax.ShapeDtypeStruct((D, D), BF),
        jax.ShapeDtypeStruct((4, D), F32),
        jax.ShapeDtypeStruct((D, FF), BF),
        jax.ShapeDtypeStruct((FF, D), BF),
        jax.ShapeDtypeStruct((experts, D), F32),
    ]
    return pl.pallas_call(
        functools.partial(bwd_kernel, groups, len(ins)),
        out_shape=outs,
        in_specs=[VMEM] * len(ins),
        out_specs=[VMEM] * len(outs),
        scratch_shapes=[
            pltpu.VMEM((images, ROWS, D), F32),
            pltpu.VMEM((images, ROWS, D), BF),
            pltpu.VMEM((images, ROWS, D), BF),
            pltpu.VMEM((images, ROWS, FF), BF),
        ],
        compiler_params=pltpu.CompilerParams(vmem_limit_bytes=60 << 20),
        name="dense_backward",
    )(*ins)


def from_peer(array, groups, shift):
    return lax.ppermute(array, "exp", [(i, (i + shift) % groups) for i in range(groups)])


def pad_images(rows, value=0):
    rows = rows.reshape(-1, PATCHES, rows.shape[-1])
    return jnp.pad(rows, ((0, 0), (0, ROWS - PATCHES), (0, 0)), constant_values=value)


def shards(
    tokens, routes, norm_gains, attn_qkv, attn_out, mlp_in, mlp_out, router, experts_in, experts_out, cotangent
):
    row_count = tokens.shape[0]
    groups = lax.axis_size("exp")
    local = experts_in.shape[0]
    choices = routes.shape[1]
    capacity = 2 * choices * row_count // (local * groups)
    images = row_count // PATCHES
    n_tok = images * ROWS
    x0, cot = pad_images(tokens), pad_images(cotangent)
    routes_t = pad_images(routes, -1).reshape(n_tok, choices).T
    routes_t = jnp.pad(routes_t, ((0, 8 - choices), (0, 0)), constant_values=-1)
    router_t = router.T
    flat = cot.reshape(n_tok, D)
    gs = [flat] + [from_peer(flat, groups, k) for k in range(1, groups)]
    rs = [routes_t] + [from_peer(routes_t, groups, k) for k in range(1, groups)]
    x1, x2, x3, qkv1, qkv2, o1, o2, p1, p2, u, gp, c = dense_forward(
        x0, norm_gains, attn_qkv, attn_out, mlp_in, mlp_out
    )
    c_flat = c.reshape(n_tok, D)
    cs = [c_flat] + [from_peer(c_flat, groups, k) for k in range(1, groups)]
    eg, ys, ds, deltas = experts_all(cs, gs, rs, router_t, experts_in, experts_out, local * capacity * groups)

    def back(parts):
        return [parts[0]] + [from_peer(parts[k], groups, groups - k) for k in range(1, groups)]

    ds, deltas, ys = back(ds), back(deltas), back(ys)
    ys = [y.reshape(images, ROWS, D) for y in ys]
    ds = [d.reshape(images, ROWS, D) for d in ds]
    rep = lax.axis_size("rep")
    eg = lax.psum_scatter(eg, "rep", scatter_dimension=2, tiled=True)
    act, gin, dqkv_a, dqkv_b, dproj_a, dproj_b, dgain, dwin, dwout, drouter = dense_backward(
        (norm_gains, attn_qkv, attn_out, mlp_in, mlp_out, router_t),
        (x0, x1, x2, x3, qkv1, qkv2, o1, o2, p1, p2, u, gp, c),
        cot, routes_t, ys, ds, deltas,
    )
    dqkv_a, dqkv_b, dproj_a, dproj_b, dwin, dwout, dgain, drouter = lax.psum(
        (dqkv_a, dqkv_b, dproj_a, dproj_b, dwin, dwout, dgain, drouter), ("rep", "exp")
    )
    return (
        act[:, :PATCHES].reshape(row_count, D),
        gin[:, :PATCHES].reshape(row_count, D),
        jnp.stack([dqkv_a, dqkv_b]).astype(F32),
        jnp.stack([dproj_a, dproj_b]).astype(F32),
        dgain,
        dwin.astype(F32),
        dwout.astype(F32),
        drouter.T,
        jnp.swapaxes(eg[:, 0], 1, 2).astype(F32),
        eg[:, 1].astype(F32),
    )


def solution(mesh):
    rows = P(("rep", "exp"), None)
    return jax.shard_map(
        shards,
        mesh=mesh,
        in_specs=(rows, rows, P(), P(), P(), P(), P(), P(), P("exp", None, None), P("exp", None, None), rows),
        out_specs=(rows, rows, P(), P(), P(), P(), P(), P(), P("exp", None, "rep"), P("exp", "rep", None)),
        check_vma=False,
    )
```

time: 655 us -> 400 us (0.61); the launches traced: 645 us -> 405 us
  matrix products: 190 us -> 0 us
  local copies, waits for them, and re-layouts: 171 us -> 8.3 us
  Pallas kernels: 0 us -> 119 us
  other arithmetic: 61.1 us -> 9.88 us
  waiting for transfers between devices: 139 us -> 178 us
  blocking collectives: 44.7 us -> 55 us
    dot_general x39 -> x0, matrix products: 190 us -> none  [the longest x1 49.2 us: shards(): jnp.einsum('sicd,idf->sicf', incoming, experts_in, preferred_element_type...]
    pallas_call x0 -> x3, Pallas kernels: none -> 119 us  [the longest x1 53.9 us: experts_all(): pl.pallas_call(functools.partial(experts_kernel, groups, local, 'exp'), g...]
    reshape x17 -> x6, local copies, waits for them, and re-layouts: 42.1 us -> 3.77 us  [the longest x3 1.54 us: pad_images(): rows = rows.reshape(-1, PATCHES, rows.shape[-1])]
    ppermute x0 -> x6, waiting for transfers between devices: none -> 35.4 us  [from_peer(): lax.ppermute(array, 'exp', [(i, (i + shift) % groups) for i in range(grou...]
    unnamed x236 -> x38, local copies, waits for them, and re-layouts: 38.7 us -> 3.41 us
    convert_element_type x12 -> x0, local copies, waits for them, and re-layouts: 34.7 us -> none  [the longest x4 18 us: attend_backward(): grad_qkv = jnp.stack([grad_query, grad_key, grad_value], axis=2).reshape(...]
    reduce_sum x18 -> x0, other arithmetic: 25.1 us -> none  [the longest x1 10.7 us: shards(): grad_gates = jnp.sum(pair_out * grad_four[:, None, :], axis=-1)]
    all_to_all x4 -> x0, starting transfers between devices: 20.8 us -> none  [the longest x1 5.48 us: shards(): lax.all_to_all(outgoing, 'exp', split_axis=0, concat_axis=0, tiled=True)]
  transfers between devices with their start and end apart: 7 -> 8, of which waited for: 1 -> 3; matrix products, arithmetic and copies ran while one was open for 44% -> 3% of each run, Pallas kernels for 0% -> 6%
where the time goes in v1:
time: 400 us; the launch traced here: 405 us
  waiting for transfers between devices  178 us (44%)
  Pallas kernels  119 us (30%)
  blocking collectives  55 us (14%)
  starting transfers between devices  18.8 us (5%)
  between operations  15.7 us (4%)
  other arithmetic  9.88 us (2%)
  local copies, waits for them, and re-layouts  8.3 us (2%)
    psum x1, waiting for transfers between devices, shards(): lax.psum((dqkv_a, dqkv_b, dproj_a, dproj_b, dwin, dwout, dgain, drouter),...  142 us
    psum x1, blocking collectives, shards(): lax.psum((dqkv_a, dqkv_b, dproj_a, dproj_b, dwin, dwout, dgain, drouter),...  55 us
    pallas_call x1, Pallas kernels, experts_all(): pl.pallas_call(functools.partial(experts_kernel, groups, local, 'exp'), g...  53.9 us
    pallas_call x1, Pallas kernels, dense_backward(): pl.pallas_call(functools.partial(bwd_kernel, groups, len(ins)), out_shape...  42 us
    ppermute x6, waiting for transfers between devices, from_peer(): lax.ppermute(array, 'exp', [(i, (i + shift) % groups) for i in range(grou...  35.4 us
    pallas_call x1, Pallas kernels, dense_forward(): pl.pallas_call(fwd_kernel, grid=(n // ib,), out_shape=outs, in_specs=[blo...  23.5 us
    ppermute x6, starting transfers between devices, from_peer(): lax.ppermute(array, 'exp', [(i, (i + shift) % groups) for i in range(grou...  18.7 us
  transfers between devices with their start and end apart: 8, of which 3 were waited for; matrix products, arithmetic and copies ran while one was open for 3% of the time, Pallas kernels for 6%

profile of v1, /device:TPU:0, one launch (start us, length us, event | category | flops | bytes accessed | tf_op | source)
XLA Modules:
  0.0 405.4 jit_solution(7172729816724640188)
XLA Ops:
  8.0 0.0 copy-start.9
  8.0 0.0 all-reduce.8.cloned.1.call-start
  8.1 1.3 reshape.61
  9.4 0.1 pad.16.refs_19_
  9.4 0.0 copy-start
  9.4 3.0 collective-permute-start.1
  12.5 0.0 copy-done.9
  12.5 0.2 reshape.60
  12.6 0.9 pad.15.x_ref.refs_6_
  13.5 23.5 %dense_forward.1 = (f32[4,208,384]{2,1,0:T(8,128)}, f32[4,208,384]{2,1,0:T(8,128)}, f32[4,208,384]{2,1,0:T(8,128)}, bf16[4,208,1152]{2,1,0:T(8,128)(2,1)}, bf16[...) custom-call(bf16[4,208,384]{2,1,0:T(8,128)(2,1)} %pad.15.x_ref.refs_, ...), custom_call_target="tpu_custom_call" | custom-call | tf_op jit(solution)/shard_map/dense_forward/pallas_call | solution.py:122
  37.0 0.0 copy-done
  37.0 0.1 collective-permute-start
  37.1 0.0 copy-done.17
  37.1 0.1 reshape.62
  37.2 0.1 reshape.63
  37.3 0.0 copy-start.13
  37.3 2.1 collective-permute-start.2
  39.4 14.4 %collective-permute-done.2.refs_5_ = s32[8,832]{1,0:T(8,128)S(1)} collective-permute-done((s32[8,832]{1,0:T(8,128)S(1)}, s32[8,832]{1,0:T(8,128)S(1)}, u32[]{:S(2)}, u32[]{:S(2)}) %collective-permute-start.2) | collective-permute-done | bytes 26656 | tf_op jit(solution)/shard_map/ppermute | solution.py:455
  53.7 0.0 collective-permute-done.1.refs_3_
  53.7 0.0 collective-permute-done.refs_1_
  53.8 0.0 copy-start.8
  53.8 0.0 copy-done.13
  53.8 0.6 copy-done.15
  54.3 0.3 copy-done.7
  54.6 0.2 copy-done.8
  54.8 53.9 %experts.1 = (bf16[4,2,1536,384]{3,2,1,0:T(8,128)(2,1)}, bf16[832,384]{1,0:T(8,128)(2,1)}, bf16[832,384]{1,0:T(8,128)(2,1)}, bf16[832,384]{1,0:T(8,128)(2,1)}, b...) custom-call(bf16[832,384]{1,0:T(8,128)(2,1)} %bitcast.32, bf16[832,384]{1,0:T(8,128)(2,1)} %copy-done.8, ...), custom_call_target="tpu_custom_call" | custom-call | tf_op jit(solution)/shard_map/experts/pallas_call | solution.py:287
  108.7 11.5 %collective-permute-start.3 = (bf16[832,384]{1,0:T(8,128)(2,1)}, bf16[832,384]{1,0:T(8,128)(2,1)S(1)}, u32[]{:S(2)}, u32[]{:S(2)}) collective-permute-start(bf16[832,384]{1,0:T(8,128)(2,1)} %get-tuple-element.52), channel_id=1, source_target_pairs={{0,1},{1,0},{2,3},{3,2},{4,5},{5,4},{6,7},{7,6},{8,9},{9,8},{10,11... | collective-permute-start | bytes 1916936 | tf_op jit(solution)/shard_map/ppermute | solution.py:455
  120.1 0.1 collective-permute-start.4
  120.2 1.9 collective-permute-start.5
  122.2 21.0 %collective-permute-done.5.refs_26_ = f32[8,832]{1,0:T(8,128)S(1)} collective-permute-done((f32[8,832]{1,0:T(8,128)}, f32[8,832]{1,0:T(8,128)S(1)}, u32[]{:S(2)}, u32[]{:S(2)}) %collective-permute-start.5) | collective-permute-done | bytes 26656 | tf_op jit(solution)/shard_map/ppermute | solution.py:455
  143.2 0.0 collective-permute-done.3
  143.2 0.0 collective-permute-done.4
  143.2 0.0 copy-start.6
  143.2 0.6 copy-done.14
  143.8 0.2 copy-done.5
  144.1 0.2 copy-done.6
  144.3 42.0 %dense_backward.1 = (bf16[4,208,384]{2,1,0:T(8,128)(2,1)}, f32[4,208,384]{2,1,0:T(8,128)}, bf16[384,1152]{1,0:T(8,128)(2,1)}, bf16[384,1152]{1,0:T(8,128)(2,1)},...) custom-call(f32[4,384]{1,0:T(4,128)} %refs_0_.1, ...), custom_call_target="tpu_custom_call" | custom-call | tf_op jit(solution)/shard_map/dense_backward/pallas_call | solution.py:438
  186.3 0.0 all-reduce.8.cloned.1.call-update
  186.3 0.0 reduce-scatter.2.cloned.1.call-start
  186.3 0.0 copy-start.10
  186.4 0.5 reduce-scatter.2.cloned.1.call-update
  186.9 0.0 copy-start.1
  186.9 0.5 copy-done.10
  187.4 0.1 slice.12
  187.5 1.0 reshape.70
  188.5 0.0 copy-done.1
  188.5 0.1 slice.13
  188.6 0.0 copy-start.16
  188.6 0.0 copy-start.18
  188.6 1.2 reshape.71
  189.8 0.0 copy-done.16
  189.8 0.0 copy-done.18
  189.8 55.0 %all-reduce.4 = (f32[4,384]{1,0:T(4,128)}, f32[384,8]{0,1:T(8,128)}) all-reduce(f32[4,384]{1,0:T(4,128)S(1)} %copy-done.18, f32[384,8]{0,1:T(8,128)S(1)} %bitcast.44), channel_id=1, replica_groups=mesh['rep'=16,'exp'=2] {'rep','exp'}, use_global_device_ids=true, to_apply=%region_4.5 | all-reduce | flops 4608 | bytes 36864 | tf_op jit(solution)/shard_map/psum | solution.py:500
  244.8 142.5 %all-reduce.8.cloned.1.call-done = (bf16[1,384,1152]{2,1,0:T(8,128)(2,1)}, bf16[1,384,1152]{2,1,0:T(8,128)(2,1)}, bf16[1,384,384]{2,1,0:T(8,128)(2,1)}, bf16[1,3...) async-done(((bf16[1,384,1152]{2,1,0:T(8,128)(2,1)}, bf16[1,384,1152]{2,1,0:T(8,128)(2,1)}, bf16[1,384,384]{2,1,0:T(8,128)(2,1)}, ...) | async-done | bytes 4718608 | tf_op jit(solution)/shard_map/psum | solution.py:500
  387.3 3.1 convert_element_type.32
  390.3 0.0 copy-done.2
  390.3 1.6 convert_element_type.33
  391.9 0.0 copy-done.11
  391.9 0.0 copy-done.12
  391.9 1.1 maximum_convert_fusion.1
  393.0 0.5 copy-done.3
  393.5 0.3 copy-done.4
  393.8 2.0 maximum_convert_fusion
  395.8 2.1 fusion
  (13 shorter events, 0.0 us)
Async XLA Ops:
  8.0 4.5 %copy-start.9 = (bf16[788,384]{1,0:T(8,128)(2,1)S(1)}, bf16[788,384]{1,0:T(8,128)(2,1)}, u32[]{:S(2)}) copy-start(bf16[788,384]{1,0:T(8,128)(2,1)} %param.11) | copy-start | bytes 1815556
  8.0 379.2 %all-reduce.8.cloned.1.call-start = ((), (), s32[]{:S(2)}) async-start(), calls=%async_computation.2 | async-start | bytes 9437184 | tf_op jit(solution)/shard_map/psum | solution.py:500
  9.4 27.6 %copy-start = (bf16[4,208,384]{2,1,0:T(8,128)(2,1)}, bf16[4,208,384]{2,1,0:T(8,128)(2,1)S(1)}, u32[]{:S(2)}) copy-start(bf16[4,208,384]{2,1,0:T(8,128)(2,1)S(1)} %pad.16.refs_19_) | copy-start | bytes 1916932
  9.4 44.3 %collective-permute-start.1 = (bf16[832,384]{1,0:T(8,128)(2,1)S(1)}, bf16[832,384]{1,0:T(8,128)(2,1)S(1)}, u32[]{:S(2)}, u32[]{:S(2)}) collective-permute-start(bf16[832,384]{1,0:T(8,128)(2,1)S(1)} %bitcast.29), channel_id=1, source_target_pairs={{0,1},{1,0},{2,3},{3,2},{4,5},{5,4},{6,7},{7,6},{8,9},{9,8},{10,11... | collective-permute-start | bytes 1916936 | tf_op jit(solution)/shard_map/ppermute | solution.py:455
  13.5 23.6 %copy-start.17 = (s32[788,2]{0,1:T(2,128)S(1)}, s32[788,2]{0,1:T(2,128)}, u32[]{:S(2)}) copy-start(s32[788,2]{0,1:T(2,128)} %param.12) | copy-start | bytes 18916
  37.0 16.7 %collective-permute-start = (bf16[832,384]{1,0:T(8,128)(2,1)}, bf16[832,384]{1,0:T(8,128)(2,1)S(1)}, u32[]{:S(2)}, u32[]{:S(2)}) collective-permute-start(bf16[832,384]{1,0:T(8,128)(2,1)} %bitcast.31), channel_id=1, source_target_pairs={{0,1},{1,0},{2,3},{3,2},{4,5},{5,4},{6,7},{7,6},{8,9},{9,8},{10,11... | collective-permute-start | bytes 1916936 | tf_op jit(solution)/shard_map/ppermute | solution.py:455
  37.3 16.5 %copy-start.13 = (s32[8,832]{1,0:T(8,128)}, s32[8,832]{1,0:T(8,128)S(1)}, u32[]{:S(2)}) copy-start(s32[8,832]{1,0:T(8,128)S(1)} %pad.18.refs_4_.refs_20_) | copy-start | bytes 79876
  37.3 16.4 %collective-permute-start.2 = (s32[8,832]{1,0:T(8,128)S(1)}, s32[8,832]{1,0:T(8,128)S(1)}, u32[]{:S(2)}, u32[]{:S(2)}) collective-permute-start(s32[8,832]{1,0:T(8,128)S(1)} %pad.18.refs_4_.refs_20_), channel_id=1, source_target_pairs={{0,1},{1,0},{2,3},{3,2},{4,5},{5,4},{6,7},{7,6},{8,9},{9,8},{10,11... | collective-permute-start | bytes 79880 | tf_op jit(solution)/shard_map/ppermute | solution.py:455
  53.7 0.6 copy-start.15
  53.7 0.9 copy-start.7
  53.8 1.0 copy-start.8
  108.7 34.5 %collective-permute-start.3 = (bf16[832,384]{1,0:T(8,128)(2,1)}, bf16[832,384]{1,0:T(8,128)(2,1)S(1)}, u32[]{:S(2)}, u32[]{:S(2)}) collective-permute-start(bf16[832,384]{1,0:T(8,128)(2,1)} %get-tuple-element.52), channel_id=1, source_target_pairs={{0,1},{1,0},{2,3},{3,2},{4,5},{5,4},{6,7},{7,6},{8,9},{9,8},{10,11... | collective-permute-start | bytes 1916936 | tf_op jit(solution)/shard_map/ppermute | solution.py:455
  120.1 23.1 %collective-permute-start.4 = (bf16[832,384]{1,0:T(8,128)(2,1)}, bf16[832,384]{1,0:T(8,128)(2,1)S(1)}, u32[]{:S(2)}, u32[]{:S(2)}) collective-permute-start(bf16[832,384]{1,0:T(8,128)(2,1)} %get-tuple-element.54), channel_id=1, source_target_pairs={{0,1},{1,0},{2,3},{3,2},{4,5},{5,4},{6,7},{7,6},{8,9},{9,8},{10,11... | collective-permute-start | bytes 1916936 | tf_op jit(solution)/shard_map/ppermute | solution.py:455
  120.2 23.0 %collective-permute-start.5 = (f32[8,832]{1,0:T(8,128)}, f32[8,832]{1,0:T(8,128)S(1)}, u32[]{:S(2)}, u32[]{:S(2)}) collective-permute-start(f32[8,832]{1,0:T(8,128)} %get-tuple-element.56), channel_id=1, source_target_pairs={{0,1},{1,0},{2,3},{3,2},{4,5},{5,4},{6,7},{7,6},{8,9},{9,8},{10,11... | collective-permute-start | bytes 79880 | tf_op jit(solution)/shard_map/ppermute | solution.py:455
  143.2 0.6 copy-start.14
  143.2 0.8 copy-start.5
  143.2 1.0 copy-start.6
  186.3 209.5 %reduce-scatter.2.cloned.1.call-start = ((), (), s32[]{:S(2)}) async-start(), calls=%async_computation.1 | async-start | bytes 10027008 | tf_op jit(solution)/shard_map/reduce_scatter | solution.py:494
  186.3 1.1 copy-start.10
  186.9 1.6 copy-start.1
  188.6 1.2 copy-start.16
  188.6 1.2 copy-start.18
  387.3 3.1 copy-start.2
  390.3 1.6 copy-start.11
  390.3 1.6 copy-start.12
  391.9 1.6 copy-start.3
  391.9 1.9 copy-start.4
Sparse Core Ops, SparseCore 0:
  186.4 200.8 all-reduce.7
Sparse Core Ops, SparseCore 1:
  191.4 132.0 reduce-scatter.1

commit v2 on v1

--- a/solution.py
+++ b/solution.py
@@ -1,4 +1,5 @@
 import functools
+import math
 
 import jax
 import jax.numpy as jnp
@@ -233,8 +234,8 @@
         return 0
 
     lax.fori_loop(0, counts[step], tile, 0)
-    eg_ref[0, 0] = acc_in[...].astype(BF)
-    eg_ref[0, 1] = acc_out[...].astype(BF)
+    eg_ref[0, 0] = acc_in[...].astype(BF).reshape(eg_ref.shape[2:])
+    eg_ref[0, 1] = acc_out[...].astype(BF).reshape(eg_ref.shape[2:])
 
     @pl.when(step == local - 1)
     def _():
@@ -271,7 +272,7 @@
             delta_refs[s][...] = rows[:, s * n_tok : (s + 1) * n_tok]
 
 
-def experts_all(cs, gs, rs, router_t, win, wout, slots_most):
+def experts_all(cs, gs, rs, router_t, win, wout, slots_most, owners):
     groups = len(cs)
     local = win.shape[0]
     n_tok = cs[0].shape[0]
@@ -281,7 +282,7 @@
     def full(shape):
         return pl.BlockSpec(tuple(shape), lambda i: (0,) * len(shape))
 
-    outs = [jax.ShapeDtypeStruct((local, 2, FF, D), BF)]
+    outs = [jax.ShapeDtypeStruct((local, 2) + owners + (FF // math.prod(owners), D), BF)]
     outs += [jax.ShapeDtypeStruct((n_tok, D), BF)] * (2 * groups)
     outs += [jax.ShapeDtypeStruct((8, n_tok), F32)] * groups
     result = pl.pallas_call(
@@ -290,7 +291,7 @@
         out_shape=outs,
         in_specs=[VMEM] * (3 * groups + 1)
         + [pl.BlockSpec((1, D, FF), lambda i: (i, 0, 0)), pl.BlockSpec((1, FF, D), lambda i: (i, 0, 0))],
-        out_specs=[pl.BlockSpec((1, 2, FF, D), lambda i: (i, 0, 0, 0))] + [full(o.shape) for o in outs[1:]],
+        out_specs=[pl.BlockSpec((1,) + outs[0].shape[1:], lambda i: (i,) + (0,) * (len(outs[0].shape) - 1))] + [full(o.shape) for o in outs[1:]],
         scratch_shapes=[
             pltpu.VMEM((total, D + 128), BF),
             pltpu.VMEM((total, D), BF),
@@ -311,10 +312,10 @@
 
 
 def bwd_kernel(groups, n_in, *refs):
-    ins, outs, scr = refs[:n_in], refs[n_in : n_in + 10], refs[n_in + 10 :]
+    ins, outs, scr = refs[:n_in], refs[n_in : n_in + 5], refs[n_in + 5 :]
     (gains, wqkv, wo, win, wout, router_t, x0, x1, x2, x3, qkv1, qkv2, o1, o2, p1, p2, u, gp, c, cot, routes) = ins[:21]
     y_refs, d_refs, delta_refs = ins[21 : 21 + groups], ins[21 + groups : 21 + 2 * groups], ins[21 + 2 * groups :]
-    act, gin, dqkv_a, dqkv_b, dproj_a, dproj_b, dgain, dwin, dwout, drouter = outs
+    act, gin, shared, dgain, drouter = outs
     gv, a_scr, dbr_scr, big = scr
     images = x0.shape[0]
     m = images * ROWS
@@ -342,7 +343,7 @@
 
     dgain[3:4] = lax.fori_loop(0, images, open_image, jnp.zeros((1, D), F32))
 
-    def attend_back(layer, gain_row, x, qkv, o, p, dqkv_out, dproj_out, last):
+    def attend_back(layer, gain_row, x, qkv, o, p, at_block, last):
         gain = gains[gain_row : gain_row + 1]
 
         def image(i, _):
@@ -373,10 +374,10 @@
             return 0
 
         lax.fori_loop(0, images, image, 0)
-        dproj_out[...] = t_dot(o[...].reshape(m, D), dbr_scr[...].reshape(m, D)).astype(BF)
+        shared[at_block + 3] = t_dot(o[...].reshape(m, D), dbr_scr[...].reshape(m, D)).astype(BF)
         a_all = a_scr[...].reshape(m, D)
-        for f in range(0, 3 * D, D):
-            dqkv_out[:, f : f + D] = t_dot(a_all, big[:, :, f : f + D].reshape(m, D)).astype(BF)
+        for f in range(3):
+            shared[at_block + f] = t_dot(a_all, big[:, :, f * D : f * D + D].reshape(m, D)).astype(BF)
 
         def close(i, total):
             da = dot_t(big[i, :, 0 : 3 * D], wqkv[layer])
@@ -390,7 +391,7 @@
 
         dgain[gain_row : gain_row + 1] = lax.fori_loop(0, images, close, jnp.zeros((1, D), F32))
 
-    attend_back(1, 2, x2, qkv2, o2, p2, dqkv_b, dproj_b, False)
+    attend_back(1, 2, x2, qkv2, o2, p2, 0, False)
 
     def mlp_image(i, _):
         a_scr[i] = (norm_parts(x1[i])[0] * gains[1:2]).astype(BF)
@@ -403,9 +404,9 @@
     lax.fori_loop(0, images, mlp_image, 0)
     dm_all = dbr_scr[...].reshape(m, D)
     b_all = a_scr[...].reshape(m, D)
-    for f in range(0, FF, 512):
-        dwout[f : f + 512] = t_dot(u[:, :, f : f + 512].reshape(m, 512), dm_all).astype(BF)
-        dwin[:, f : f + 512] = t_dot(b_all, big[:, :, f : f + 512].reshape(m, 512)).astype(BF)
+    for f in range(4):
+        shared[4 + f] = t_dot(u[:, :, f * D : f * D + D].reshape(m, D), dm_all).astype(BF)
+        shared[8 + f] = t_dot(b_all, big[:, :, f * D : f * D + D].reshape(m, D)).astype(BF)
 
     def mlp_close(i, total):
         db = dot_t(big[i], win[...])
@@ -415,7 +416,7 @@
 
     dgain[1:2] = lax.fori_loop(0, images, mlp_close, jnp.zeros((1, D), F32))
 
-    attend_back(0, 0, x0, qkv1, o1, p1, dqkv_a, dproj_a, True)
+    attend_back(0, 0, x0, qkv1, o1, p1, 12, True)
 
 
 def dense_backward(weights, saved, cot, routes, ys, ds, deltas):
@@ -426,13 +427,8 @@
     outs = [
         jax.ShapeDtypeStruct((images, ROWS, D), BF),
         jax.ShapeDtypeStruct((images, ROWS, D), F32),
-        jax.ShapeDtypeStruct((D, 3 * D), BF),
-        jax.ShapeDtypeStruct((D, 3 * D), BF),
-        jax.ShapeDtypeStruct((D, D), BF),
-        jax.ShapeDtypeStruct((D, D), BF),
+        jax.ShapeDtypeStruct((16, D, D), BF),
         jax.ShapeDtypeStruct((4, D), F32),
-        jax.ShapeDtypeStruct((D, FF), BF),
-        jax.ShapeDtypeStruct((FF, D), BF),
         jax.ShapeDtypeStruct((experts, D), F32),
     ]
     return pl.pallas_call(
@@ -451,6 +447,286 @@
     )(*ins)
 
 
+OUTER, SHARE = 4, 48
+MESH = pl.DeviceIdType.MESH
+
+
+class Place:
+    def __init__(self):
+        r = lax.axis_index("rep")
+        self.y = lax.axis_index("exp")
+        self.z, self.x, self.c = r // 4, (r // 2) % 2, r % 2
+        self.core = (r + 1 - 2 * self.c, self.y)
+        self.across = (r + 2 - 4 * self.x, self.y)
+        self.beside = (r, 1 - self.y)
+        self.along = [((self.z + k) % OUTER) for k in range(1, OUTER)]
+
+    def at_z(self, z):
+        return (z * 4 + self.x * 2 + self.c, self.y)
+
+    def meet(self):
+        barrier = pltpu.get_barrier_semaphore()
+        partners = [self.core, self.across, self.beside] + [self.at_z(z) for z in self.along]
+        for partner in partners:
+            pl.semaphore_signal(barrier, inc=1, device_id=partner, device_id_type=MESH)
+        pl.semaphore_wait(barrier, len(partners))
+
+
+class Links:
+    def __init__(self, send, recv):
+        self.send, self.recv, self.used = send, recv, 0
+
+    def start(self, src, dst, device):
+        copy = pltpu.make_async_remote_copy(
+            src_ref=src, dst_ref=dst, send_sem=self.send.at[self.used], recv_sem=self.recv.at[self.used],
+            device_id=device, device_id_type=MESH,
+        )
+        self.used += 1
+        copy.start()
+        return copy
+
+
+def add_into(count, target, *others):
+    def block(i, _):
+        total = target(i)[...].astype(F32)
+        for other in others:
+            total = total + other(i)[...].astype(F32)
+        target(i)[...] = total.astype(target(i).dtype)
+        return 0
+
+    lax.fori_loop(0, count, block, 0)
+
+
+class ExpertSum:
+    COPIES = 2 + OUTER - 1
+
+    def __init__(self, place, links, j, eg, own, core_rx, x_rx, z_rx, out, local_sem):
+        self.p, self.links, self.j, self.out = place, links, j, out
+        self.eg, self.own, self.core_rx, self.x_rx, self.z_rx = eg, own, core_rx, x_rx, z_rx
+        self.sem = local_sem.at[j]
+
+    def core(self):
+        p, j = self.p, self.j
+        self.load = pltpu.make_async_copy(self.eg.at[j, :, :, :, p.c], self.own.at[j], self.sem)
+        self.load.start()
+        self.c1 = self.links.start(self.eg.at[j, :, :, :, 1 - p.c], self.core_rx.at[j], p.core)
+
+    def across(self):
+        p, j = self.p, self.j
+        self.load.wait()
+        self.c1.wait()
+        for x in (1 - p.x, p.x):
+            add_into(
+                2 * OUTER,
+                lambda i: self.own.at[j, i // OUTER, i % OUTER, x],
+                lambda i: self.core_rx.at[j, i // OUTER, i % OUTER, x],
+            )
+            if x is not p.x:
+                self.c2 = self.links.start(self.own.at[j, :, :, 1 - p.x], self.x_rx.at[j], p.across)
+
+    def along(self):
+        p, j = self.p, self.j
+        self.c2.wait()
+        add_into(
+            2 * OUTER,
+            lambda i: self.own.at[j, i // OUTER, i % OUTER, p.x],
+            lambda i: self.x_rx.at[j, i // OUTER, i % OUTER],
+        )
+        self.c3 = [
+            self.links.start(self.own.at[j, :, z, p.x], self.z_rx.at[j, k], p.at_z(z)) for k, z in enumerate(p.along)
+        ]
+
+    def finish(self):
+        p, j = self.p, self.j
+        for c in self.c3:
+            c.wait()
+        for part in range(2):
+            total = self.own[j, part, p.z, p.x].astype(F32)
+            for k in range(OUTER - 1):
+                total = total + self.z_rx[j, k, part].astype(F32)
+            self.out[j, part] = total
+
+
+class SharedSum:
+    COPIES = 2 * (3 + OUTER - 1)
+
+    def __init__(self, place, links, g, src, rx1, rx2, rx3, rx4, out):
+        self.p, self.links, self.out = place, links, out.at[g]
+        self.src, self.rx1, self.rx2, self.rx3, self.rx4 = src.at[g], rx1.at[g], rx2.at[g], rx3.at[g], rx4.at[g]
+
+    def core(self):
+        p = self.p
+        self.c = self.links.start(self.src.at[1 - p.c], self.rx1, p.core)
+
+    def beside(self):
+        p = self.p
+        self.c.wait()
+        add_into(
+            4 * OUTER,
+            lambda i: self.src.at[p.c, i // (2 * OUTER), (i // OUTER) % 2, i % OUTER],
+            lambda i: self.rx1.at[i // (2 * OUTER), (i // OUTER) % 2, i % OUTER],
+        )
+        self.c = self.links.start(self.src.at[p.c, 1 - p.y], self.rx2, p.beside)
+
+    def across(self):
+        p = self.p
+        self.c.wait()
+        add_into(
+            2 * OUTER,
+            lambda i: self.src.at[p.c, p.y, i // OUTER, i % OUTER],
+            lambda i: self.rx2.at[i // OUTER, i % OUTER],
+        )
+        self.c = self.links.start(self.src.at[p.c, p.y, 1 - p.x], self.rx3, p.across)
+
+    def along(self):
+        p = self.p
+        self.c.wait()
+        add_into(OUTER, lambda i: self.src.at[p.c, p.y, p.x, i], lambda i: self.rx3.at[i])
+        self.cs = [
+            self.links.start(self.src.at[p.c, p.y, p.x, z], self.rx4.at[k], p.at_z(z)) for k, z in enumerate(p.along)
+        ]
+
+    def out_along(self):
+        p = self.p
+        for c in self.cs:
+            c.wait()
+        total = self.src[p.c, p.y, p.x, p.z].astype(F32)
+        for k in range(OUTER - 1):
+            total = total + self.rx4[k].astype(F32)
+        mine = self.out.at[p.c, p.y, p.x, p.z]
+        mine[...] = total.astype(BF)
+        self.cs = [self.links.start(mine, mine, p.at_z(z)) for z in p.along]
+
+    def out_across(self):
+        p = self.p
+        for c in self.cs:
+            c.wait()
+        mine = self.out.at[p.c, p.y, p.x]
+        self.c = self.links.start(mine, mine, p.across)
+
+    def out_beside(self):
+        p = self.p
+        self.c.wait()
+        mine = self.out.at[p.c, p.y]
+        self.c = self.links.start(mine, mine, p.beside)
+
+    def out_core(self):
+        p = self.p
+        self.c.wait()
+        mine = self.out.at[p.c]
+        self.c = self.links.start(mine, mine, p.core)
+
+    def finish(self):
+        self.c.wait()
+
+
+class SmallSum:
+    COPIES = 3 + OUTER - 1
+
+    def __init__(self, place, links, src, rx):
+        self.p, self.links, self.src, self.rx = place, links, src, rx
+
+    def step(self, k):
+        device = (self.p.core, self.p.beside, self.p.across)[k]
+        if k:
+            self.c.wait()
+            self.src[k] = self.src[k - 1] + self.rx[k - 1]
+        self.c = self.links.start(self.src.at[k], self.rx.at[k], device)
+
+    def along(self):
+        self.c.wait()
+        self.src[3] = self.src[2] + self.rx[2]
+        self.cs = [
+            self.links.start(self.src.at[3], self.rx.at[3 + k], self.p.at_z(z)) for k, z in enumerate(self.p.along)
+        ]
+
+    def finish(self, out):
+        for c in self.cs:
+            c.wait()
+        total = self.src[3]
+        for k in range(OUTER - 1):
+            total = total + self.rx[3 + k]
+        out[...] = total
+
+
+def sums_kernel(
+    eg, sh, small, eg_out, sh_out, small_out,
+    own, core_rx, x_rx, z_rx, rx1, rx2, rx3, rx4, small_src, small_rx, local_sem, send, recv,
+):
+    place = Place()
+    links = Links(send, recv)
+    place.meet()
+    experts = [ExpertSum(place, links, j, eg, own, core_rx, x_rx, z_rx, eg_out, local_sem) for j in range(eg.shape[0])]
+    groups = [SharedSum(place, links, g, sh, rx1, rx2, rx3, rx4, sh_out) for g in range(sh.shape[0])]
+    few = SmallSum(place, links, small_src, small_rx)
+    small_src[0] = small[...]
+    few.step(0)
+    for e in experts:
+        e.core()
+    for g in groups:
+        g.core()
+    for e in experts:
+        e.across()
+    few.step(1)
+    for g in groups:
+        g.beside()
+    few.step(2)
+    for g in groups:
+        g.across()
+    few.along()
+    for e in experts:
+        e.along()
+    for g in groups:
+        g.along()
+    few.finish(small_out)
+    for g in groups:
+        g.out_along()
+    for e in experts:
+        e.finish()
+    for g in groups:
+        g.out_across()
+    for g in groups:
+        g.out_beside()
+    for g in groups:
+        g.out_core()
+    for g in groups:
+        g.finish()
+
+
+def device_sums(eg, sh, small):
+    local, groups = eg.shape[0], sh.shape[0]
+    copies = local * ExpertSum.COPIES + groups * SharedSum.COPIES + SmallSum.COPIES
+    share = eg.shape[-2]
+    vm = pltpu.VMEM
+    return pl.pallas_call(
+        sums_kernel,
+        out_shape=[
+            jax.ShapeDtypeStruct((local, 2, share, D), F32),
+            jax.ShapeDtypeStruct(sh.shape, BF),
+            jax.ShapeDtypeStruct(small.shape, F32),
+        ],
+        in_specs=[pl.BlockSpec(memory_space=pl.ANY), VMEM, VMEM],
+        out_specs=[VMEM] * 3,
+        scratch_shapes=[
+            vm((local, 2, OUTER, 2, share, D), BF),
+            vm((local, 2, OUTER, 2, share, D), BF),
+            vm((local, 2, OUTER, share, D), BF),
+            vm((local, OUTER - 1, 2, share, D), BF),
+            vm((groups, 2, 2, OUTER, SHARE, D), BF),
+            vm((groups, 2, OUTER, SHARE, D), BF),
+            vm((groups, OUTER, SHARE, D), BF),
+            vm((groups, OUTER - 1, SHARE, D), BF),
+            vm((4,) + small.shape, F32),
+            vm((OUTER + 2,) + small.shape, F32),
+            pltpu.SemaphoreType.DMA((local,)),
+            pltpu.SemaphoreType.DMA((copies,)),
+            pltpu.SemaphoreType.DMA((copies,)),
+        ],
+        compiler_params=pltpu.CompilerParams(collective_id=1, has_side_effects=True, vmem_limit_bytes=60 << 20),
+        name="sums",
+    )(eg, sh, small)
+
+
 def from_peer(array, groups, shift):
     return lax.ppermute(array, "exp", [(i, (i + shift) % groups) for i in range(groups)])
 
@@ -458,6 +734,10 @@
 def pad_images(rows, value=0):
     rows = rows.reshape(-1, PATCHES, rows.shape[-1])
     return jnp.pad(rows, ((0, 0), (0, ROWS - PATCHES), (0, 0)), constant_values=value)
+
+
+def side_by_side(blocks):
+    return jnp.swapaxes(blocks, 0, 1).reshape(D, -1)
 
 
 def shards(
@@ -482,7 +762,12 @@
     )
     c_flat = c.reshape(n_tok, D)
     cs = [c_flat] + [from_peer(c_flat, groups, k) for k in range(1, groups)]
-    eg, ys, ds, deltas = experts_all(cs, gs, rs, router_t, experts_in, experts_out, local * capacity * groups)
+    rep = lax.axis_size("rep")
+    known = (rep, groups, local) == (16, 2, 4)
+    owners = (OUTER, 2, 2) if known else (rep,)
+    eg, ys, ds, deltas = experts_all(
+        cs, gs, rs, router_t, experts_in, experts_out, local * capacity * groups, owners
+    )
 
     def back(parts):
         return [parts[0]] + [from_peer(parts[k], groups, groups - k) for k in range(1, groups)]
@@ -490,27 +775,32 @@
     ds, deltas, ys = back(ds), back(deltas), back(ys)
     ys = [y.reshape(images, ROWS, D) for y in ys]
     ds = [d.reshape(images, ROWS, D) for d in ds]
-    rep = lax.axis_size("rep")
-    eg = lax.psum_scatter(eg, "rep", scatter_dimension=2, tiled=True)
-    act, gin, dqkv_a, dqkv_b, dproj_a, dproj_b, dgain, dwin, dwout, drouter = dense_backward(
+    act, gin, shared, dgain, drouter = dense_backward(
         (norm_gains, attn_qkv, attn_out, mlp_in, mlp_out, router_t),
         (x0, x1, x2, x3, qkv1, qkv2, o1, o2, p1, p2, u, gp, c),
         cot, routes_t, ys, ds, deltas,
     )
-    dqkv_a, dqkv_b, dproj_a, dproj_b, dwin, dwout, dgain, drouter = lax.psum(
-        (dqkv_a, dqkv_b, dproj_a, dproj_b, dwin, dwout, dgain, drouter), ("rep", "exp")
-    )
+    experts = drouter.shape[0]
+    small = jnp.concatenate([dgain, drouter], axis=0)
+    if known:
+        small = jnp.pad(small, ((0, 16 - small.shape[0]), (0, 0)))
+        eg, shared, small = device_sums(eg, shared.reshape(4, 2, 2, 2, OUTER, SHARE, D), small)
+        shared = shared.reshape(16, D, D)
+    else:
+        eg = lax.psum_scatter(eg, "rep", scatter_dimension=2, tiled=True).reshape(local, 2, FF // rep, D).astype(F32)
+        shared, small = lax.psum((shared, small), ("rep", "exp"))
+    shared = shared.astype(F32)
     return (
         act[:, :PATCHES].reshape(row_count, D),
         gin[:, :PATCHES].reshape(row_count, D),
-        jnp.stack([dqkv_a, dqkv_b]).astype(F32),
-        jnp.stack([dproj_a, dproj_b]).astype(F32),
-        dgain,
-        dwin.astype(F32),
-        dwout.astype(F32),
-        drouter.T,
-        jnp.swapaxes(eg[:, 0], 1, 2).astype(F32),
-        eg[:, 1].astype(F32),
+        jnp.stack([side_by_side(shared[12:15]), side_by_side(shared[0:3])]),
+        jnp.stack([shared[15], shared[3]]),
+        small[0:4],
+        side_by_side(shared[8:12]),
+        shared[4:8].reshape(FF, D),
+        small[4 : 4 + experts].T,
+        jnp.swapaxes(eg[:, 0], 1, 2),
+        eg[:, 1],
     )
 
 

time: 400 us -> 399 us (level)
  Pallas kernels: 119 us -> 316 us
  waiting for transfers between devices: 178 us -> 41.7 us
  blocking collectives: 55 us -> 0 us
  local copies, waits for them, and re-layouts: 8.3 us -> 30.7 us
  between operations: 15.7 us -> 0.8 us
  starting transfers between devices: 18.8 us -> 7.35 us
    pallas_call x0 -> x1, Pallas kernels: none -> 177 us  [device_sums(): pl.pallas_call(sums_kernel, out_shape=[jax.ShapeDtypeStruct((local, 2, sh...]
    psum x1 -> x0, waiting for transfers between devices: 142 us -> none  [shards(): lax.psum((dqkv_a, dqkv_b, dproj_a, dproj_b, dwin, dwout, dgain, drouter),...]
    psum x1 -> x0, blocking collectives: 55 us -> none  [shards(): lax.psum((dqkv_a, dqkv_b, dproj_a, dproj_b, dwin, dwout, dgain, drouter),...]
    pallas_call x1, Pallas kernels: 53.9 us -> 73.3 us  [experts_all(): pl.pallas_call(functools.partial(experts_kernel, groups, local, 'exp'), g...]
    ppermute x6, starting transfers between devices: 18.7 us -> 7.35 us  [from_peer(): lax.ppermute(array, 'exp', [(i, (i + shift) % groups) for i in range(grou...]
    convert_element_type x5 -> x1, other arithmetic: 9.88 us -> 1.18 us  [shards(): shared = shared.astype(F32)]
    slice x0 -> x4, local copies, waits for them, and re-layouts: none -> 8.15 us  [the longest x1 3.67 us: shards(): shared[4:8].reshape(FF, D)]
    unnamed x38 -> x31, local copies, waits for them, and re-layouts: 3.41 us -> 9.81 us
  transfers between devices with their start and end apart: 8 -> 6, of which waited for: 3 -> 2; matrix products, arithmetic and copies ran while one was open for 3% -> 0% of each run, Pallas kernels for 6% -> 6%
where the time goes in v2:
time: 399 us; the launch traced here: 404 us
  Pallas kernels  316 us (79%)
  waiting for transfers between devices  41.7 us (10%)
  local copies, waits for them, and re-layouts  30.7 us (8%)
  starting transfers between devices  7.35 us (2%)
  other arithmetic  7.07 us (2%)
    pallas_call x1, Pallas kernels, device_sums(): pl.pallas_call(sums_kernel, out_shape=[jax.ShapeDtypeStruct((local, 2, sh...  177 us
    pallas_call x1, Pallas kernels, experts_all(): pl.pallas_call(functools.partial(experts_kernel, groups, local, 'exp'), g...  73.3 us
    pallas_call x1, Pallas kernels, dense_backward(): pl.pallas_call(functools.partial(bwd_kernel, groups, len(ins)), out_shape...  42.6 us
    ppermute x6, waiting for transfers between devices, from_peer(): lax.ppermute(array, 'exp', [(i, (i + shift) % groups) for i in range(grou...  41.7 us
    pallas_call x1, Pallas kernels, dense_forward(): pl.pallas_call(fwd_kernel, grid=(n // ib,), out_shape=outs, in_specs=[blo...  23.4 us
    unnamed x31, local copies, waits for them, and re-layouts  9.81 us
  transfers between devices with their start and end apart: 6, of which 2 were waited for; matrix products, arithmetic and copies ran while one was open for 0% of the time, Pallas kernels for 6%

profile of v2, /device:TPU:0, one launch (start us, length us, event | category | flops | bytes accessed | tf_op | source)
XLA Modules:
  0.0 403.9 jit_solution(10429243974022257199)
XLA Ops:
  0.6 0.0 copy-start.8
  0.7 1.3 reshape.71
  2.0 0.1 pad.20.refs_19_
  2.0 0.0 copy-start.2
  2.0 3.0 collective-permute-start.1
  5.1 0.0 copy-done.8
  5.1 0.2 reshape.70
  5.2 0.9 pad.19.x_ref.refs_6_
  6.1 0.0 copy-start.13
  6.1 23.4 %dense_forward.1 = (f32[4,208,384]{2,1,0:T(8,128)}, f32[4,208,384]{2,1,0:T(8,128)}, f32[4,208,384]{2,1,0:T(8,128)}, bf16[4,208,1152]{2,1,0:T(8,128)(2,1)}, bf16[...) custom-call(bf16[4,208,384]{2,1,0:T(8,128)(2,1)} %pad.19.x_ref.refs_, ...), custom_call_target="tpu_custom_call" | custom-call | tf_op jit(solution)/shard_map/dense_forward/pallas_call | solution.py:123
  29.6 0.0 copy-done.2
  29.6 0.1 collective-permute-start
  29.7 0.0 copy-done.13
  29.7 0.1 reshape.72
  29.8 0.1 reshape.73
  29.9 0.0 copy-start.10
  29.9 2.1 collective-permute-start.2
  31.9 14.4 %collective-permute-done.2.refs_5_ = s32[8,832]{1,0:T(8,128)S(1)} collective-permute-done((s32[8,832]{1,0:T(8,128)S(1)}, s32[8,832]{1,0:T(8,128)S(1)}, u32[]{:S(2)}, u32[]{:S(2)}) %collective-permute-start.2) | collective-permute-done | bytes 26656 | tf_op jit(solution)/shard_map/ppermute | solution.py:731
  46.3 0.0 copy-start.12
  46.3 0.0 collective-permute-done.1.refs_3_
  46.3 0.0 copy-start.6
  46.3 0.0 collective-permute-done.refs_1_
  46.3 0.0 copy-start.7
  46.3 0.0 copy-done.10
  46.3 0.6 copy-done.12
  46.9 0.2 copy-done.6
  47.1 0.2 copy-done.7
  47.4 73.3 %experts.1 = (bf16[4,2,4,2,2,96,384]{6,5,4,3,2,1,0:T(8,128)(2,1)}, bf16[832,384]{1,0:T(8,128)(2,1)}, bf16[832,384]{1,0:T(8,128)(2,1)}, bf16[832,384]{1,0:T(8,128...) custom-call(bf16[832,384]{1,0:T(8,128)(2,1)} %bitcast.43, bf16[832,384]{1,0:T(8,128)(2,1)} %copy-done.7, ...), custom_call_target="tpu_custom_call" | custom-call | tf_op jit(solution)/shard_map/experts/pallas_call | solution.py:288
  120.7 0.1 collective-permute-start.3
  120.7 2.0 collective-permute-start.4
  122.8 0.1 collective-permute-start.5
  122.8 27.4 %collective-permute-done.5.refs_26_ = f32[8,832]{1,0:T(8,128)S(1)} collective-permute-done((f32[8,832]{1,0:T(8,128)}, f32[8,832]{1,0:T(8,128)S(1)}, u32[]{:S(2)}, u32[]{:S(2)}) %collective-permute-start.5) | collective-permute-done | bytes 26656 | tf_op jit(solution)/shard_map/ppermute | solution.py:731
  150.2 0.0 copy-start.11
  150.2 0.0 collective-permute-done.3
  150.2 0.0 copy-start.4
  150.2 0.0 collective-permute-done.4
  150.2 0.0 copy-start.5
  150.2 0.6 copy-done.11
  150.8 0.2 copy-done.4
  151.0 0.2 copy-done.5
  151.3 42.6 %dense_backward.1 = (bf16[4,208,384]{2,1,0:T(8,128)(2,1)}, f32[4,208,384]{2,1,0:T(8,128)}, bf16[16,384,384]{2,1,0:T(8,128)(2,1)}, f32[4,384]{1,0:T(4,128)}, f32[8,384]{1,0:T(8,128)}) custom-call(f32[4,384]{1,0:T(4,128)} %refs_0_.1, bf16[2,384,1152]{2,1,0:T(8,128)(2,1)} %refs_1_.1, bf16[2,384,384]{2,1,0:T(8,128)(2,1)} %refs_2_.1, bf16[384,1536]{1,0:T(8,128)(2,1)} %refs_3_.1, ...), custom_call_target="tpu_custom_call" | custom-call | tf_op jit(solution)/shard_map/dense_backward/pallas_call | solution.py:434
  193.9 1.3 select_maximum_fusion.small
  195.2 176.9 %sums.1 = (f32[4,2,96,384]{3,2,1,0:T(8,128)}, bf16[4,2,2,2,4,48,384]{6,5,4,3,2,1,0:T(8,128)(2,1)}, f32[16,384]{1,0:T(8,128)}) custom-call(bf16[4,2,4,2,2,96,384]{6,5,4,3,2,1,0:T(8,128)(2,1)} %get-tuple-element.57.eg, bf16[4,2,2,2,4,48,384]{6,5,4,3,2,1,0:T(8,128)(2,1)} %bitcast.41, f32[16,384]{1,0:T(8,128)} %select_maximum_fusion.small), custom_call_target="tpu_custom_call" | custom-call | tf_op jit(solution)/shard_map/sums/pallas_call | solution.py:701
  372.1 1.3 slice.46
  373.4 1.3 slice_bitcast_fusion.2
  374.8 3.7 fusion.2
  378.5 0.0 copy-done
  378.5 1.2 convert_element_type.11
  379.6 1.1 fusion
  380.8 2.1 fusion.1
  382.8 0.0 copy-done.9
  382.8 0.1 slice.40
  382.9 1.0 reshape.80
  383.9 2.4 slice_bitcast_fusion
  386.3 0.0 copy-done.3
  386.3 1.1 slice.41
  387.4 2.5 reshape.81
  389.9 1.7 copy.28
  391.6 3.0 copy.26
  394.6 0.0 copy-done.1
  394.6 1.8 copy.27
  396.4 2.2 pad_maximum_fusion
  398.6 2.9 copy.25
  401.6 2.3 pad_maximum_fusion.1
  (6 shorter events, 0.0 us)
Async XLA Ops:
  0.6 4.4 %copy-start.8 = (bf16[788,384]{1,0:T(8,128)(2,1)S(1)}, bf16[788,384]{1,0:T(8,128)(2,1)}, u32[]{:S(2)}) copy-start(bf16[788,384]{1,0:T(8,128)(2,1)} %param.11) | copy-start | bytes 1815556
  2.0 27.5 %copy-start.2 = (bf16[4,208,384]{2,1,0:T(8,128)(2,1)}, bf16[4,208,384]{2,1,0:T(8,128)(2,1)S(1)}, u32[]{:S(2)}) copy-start(bf16[4,208,384]{2,1,0:T(8,128)(2,1)S(1)} %pad.20.refs_19_) | copy-start | bytes 1916932
  2.0 44.3 %collective-permute-start.1 = (bf16[832,384]{1,0:T(8,128)(2,1)S(1)}, bf16[832,384]{1,0:T(8,128)(2,1)S(1)}, u32[]{:S(2)}, u32[]{:S(2)}) collective-permute-start(bf16[832,384]{1,0:T(8,128)(2,1)S(1)} %bitcast.39), channel_id=1, source_target_pairs={{0,1},{1,0},{2,3},{3,2},{4,5},{5,4},{6,7},{7,6},{8,9},{9,8},{10,11... | collective-permute-start | bytes 1916936 | tf_op jit(solution)/shard_map/ppermute | solution.py:731
  6.1 23.5 %copy-start.13 = (s32[788,2]{0,1:T(2,128)S(1)}, s32[788,2]{0,1:T(2,128)}, u32[]{:S(2)}) copy-start(s32[788,2]{0,1:T(2,128)} %param.12) | copy-start | bytes 18916
  29.6 16.7 %collective-permute-start = (bf16[832,384]{1,0:T(8,128)(2,1)}, bf16[832,384]{1,0:T(8,128)(2,1)S(1)}, u32[]{:S(2)}, u32[]{:S(2)}) collective-permute-start(bf16[832,384]{1,0:T(8,128)(2,1)} %bitcast.42), channel_id=1, source_target_pairs={{0,1},{1,0},{2,3},{3,2},{4,5},{5,4},{6,7},{7,6},{8,9},{9,8},{10,11... | collective-permute-start | bytes 1916936 | tf_op jit(solution)/shard_map/ppermute | solution.py:731
  29.9 16.5 %copy-start.10 = (s32[8,832]{1,0:T(8,128)}, s32[8,832]{1,0:T(8,128)S(1)}, u32[]{:S(2)}) copy-start(s32[8,832]{1,0:T(8,128)S(1)} %pad.22.refs_4_.refs_20_) | copy-start | bytes 79876
  29.9 16.4 %collective-permute-start.2 = (s32[8,832]{1,0:T(8,128)S(1)}, s32[8,832]{1,0:T(8,128)S(1)}, u32[]{:S(2)}, u32[]{:S(2)}) collective-permute-start(s32[8,832]{1,0:T(8,128)S(1)} %pad.22.refs_4_.refs_20_), channel_id=1, source_target_pairs={{0,1},{1,0},{2,3},{3,2},{4,5},{5,4},{6,7},{7,6},{8,9},{9,8},{10,11... | collective-permute-start | bytes 79880 | tf_op jit(solution)/shard_map/ppermute | solution.py:731
  46.3 0.6 copy-start.12
  46.3 0.8 copy-start.6
  46.3 1.0 copy-start.7
  120.7 29.5 %collective-permute-start.3 = (bf16[832,384]{1,0:T(8,128)(2,1)}, bf16[832,384]{1,0:T(8,128)(2,1)S(1)}, u32[]{:S(2)}, u32[]{:S(2)}) collective-permute-start(bf16[832,384]{1,0:T(8,128)(2,1)} %get-tuple-element.50), channel_id=1, source_target_pairs={{0,1},{1,0},{2,3},{3,2},{4,5},{5,4},{6,7},{7,6},{8,9},{9,8},{10,11... | collective-permute-start | bytes 1916936 | tf_op jit(solution)/shard_map/ppermute | solution.py:731
  120.7 29.5 %collective-permute-start.4 = (bf16[832,384]{1,0:T(8,128)(2,1)}, bf16[832,384]{1,0:T(8,128)(2,1)S(1)}, u32[]{:S(2)}, u32[]{:S(2)}) collective-permute-start(bf16[832,384]{1,0:T(8,128)(2,1)} %get-tuple-element.52), channel_id=1, source_target_pairs={{0,1},{1,0},{2,3},{3,2},{4,5},{5,4},{6,7},{7,6},{8,9},{9,8},{10,11... | collective-permute-start | bytes 1916936 | tf_op jit(solution)/shard_map/ppermute | solution.py:731
  122.8 27.4 %collective-permute-start.5 = (f32[8,832]{1,0:T(8,128)}, f32[8,832]{1,0:T(8,128)S(1)}, u32[]{:S(2)}, u32[]{:S(2)}) collective-permute-start(f32[8,832]{1,0:T(8,128)} %get-tuple-element.54), channel_id=1, source_target_pairs={{0,1},{1,0},{2,3},{3,2},{4,5},{5,4},{6,7},{7,6},{8,9},{9,8},{10,11... | collective-permute-start | bytes 79880 | tf_op jit(solution)/shard_map/ppermute | solution.py:731
  150.2 0.6 copy-start.11
  150.2 0.8 copy-start.4
  150.2 1.1 copy-start.5
  374.8 3.7 copy-start
  380.8 2.1 copy-start.9
  383.9 2.4 copy-start.3
  391.6 3.0 copy-start.1

commit v3 on v1

--- a/solution.py
+++ b/solution.py
@@ -1,4 +1,5 @@
 import functools
+import math
 
 import jax
 import jax.numpy as jnp
@@ -233,8 +234,8 @@
         return 0
 
     lax.fori_loop(0, counts[step], tile, 0)
-    eg_ref[0, 0] = acc_in[...].astype(BF)
-    eg_ref[0, 1] = acc_out[...].astype(BF)
+    eg_ref[0, 0] = acc_in[...].astype(BF).reshape(eg_ref.shape[2:])
+    eg_ref[0, 1] = acc_out[...].astype(BF).reshape(eg_ref.shape[2:])
 
     @pl.when(step == local - 1)
     def _():
@@ -271,7 +272,7 @@
             delta_refs[s][...] = rows[:, s * n_tok : (s + 1) * n_tok]
 
 
-def experts_all(cs, gs, rs, router_t, win, wout, slots_most):
+def experts_all(cs, gs, rs, router_t, win, wout, slots_most, owners):
     groups = len(cs)
     local = win.shape[0]
     n_tok = cs[0].shape[0]
@@ -281,7 +282,7 @@
     def full(shape):
         return pl.BlockSpec(tuple(shape), lambda i: (0,) * len(shape))
 
-    outs = [jax.ShapeDtypeStruct((local, 2, FF, D), BF)]
+    outs = [jax.ShapeDtypeStruct((local, 2) + owners + (FF // math.prod(owners), D), BF)]
     outs += [jax.ShapeDtypeStruct((n_tok, D), BF)] * (2 * groups)
     outs += [jax.ShapeDtypeStruct((8, n_tok), F32)] * groups
     result = pl.pallas_call(
@@ -290,7 +291,7 @@
         out_shape=outs,
         in_specs=[VMEM] * (3 * groups + 1)
         + [pl.BlockSpec((1, D, FF), lambda i: (i, 0, 0)), pl.BlockSpec((1, FF, D), lambda i: (i, 0, 0))],
-        out_specs=[pl.BlockSpec((1, 2, FF, D), lambda i: (i, 0, 0, 0))] + [full(o.shape) for o in outs[1:]],
+        out_specs=[pl.BlockSpec((1,) + outs[0].shape[1:], lambda i: (i,) + (0,) * (len(outs[0].shape) - 1))] + [full(o.shape) for o in outs[1:]],
         scratch_shapes=[
             pltpu.VMEM((total, D + 128), BF),
             pltpu.VMEM((total, D), BF),
@@ -310,154 +311,625 @@
     return result[0], result[1 : groups + 1], result[groups + 1 : 2 * groups + 1], result[2 * groups + 1 :]
 
 
-def bwd_kernel(groups, n_in, *refs):
-    ins, outs, scr = refs[:n_in], refs[n_in : n_in + 10], refs[n_in + 10 :]
-    (gains, wqkv, wo, win, wout, router_t, x0, x1, x2, x3, qkv1, qkv2, o1, o2, p1, p2, u, gp, c, cot, routes) = ins[:21]
-    y_refs, d_refs, delta_refs = ins[21 : 21 + groups], ins[21 + groups : 21 + 2 * groups], ins[21 + 2 * groups :]
-    act, gin, dqkv_a, dqkv_b, dproj_a, dproj_b, dgain, dwin, dwout, drouter = outs
-    gv, a_scr, dbr_scr, big = scr
-    images = x0.shape[0]
+OUTER, SHARE = 4, 48
+MESH = pl.DeviceIdType.MESH
+
+
+class Place:
+    def __init__(self):
+        r = lax.axis_index("rep")
+        self.y = lax.axis_index("exp")
+        self.z, self.x, self.c = r // 4, (r // 2) % 2, r % 2
+        self.core = (r + 1 - 2 * self.c, self.y)
+        self.across = (r + 2 - 4 * self.x, self.y)
+        self.beside = (r, 1 - self.y)
+        self.along = [((self.z + k) % OUTER) for k in range(1, OUTER)]
+
+    def at_z(self, z):
+        return (z * 4 + self.x * 2 + self.c, self.y)
+
+    def meet(self, partners):
+        barrier = pltpu.get_barrier_semaphore()
+        for partner in partners:
+            pl.semaphore_signal(barrier, inc=1, device_id=partner, device_id_type=MESH)
+        pl.semaphore_wait(barrier, len(partners))
+
+
+class Links:
+    def __init__(self, send, recv):
+        self.send, self.recv, self.used = send, recv, 0
+
+    def reserve(self, count):
+        first = self.used
+        self.used += count
+        return first
+
+    def copy(self, at, src, dst, device):
+        return pltpu.make_async_remote_copy(
+            src_ref=src, dst_ref=dst, send_sem=self.send.at[at], recv_sem=self.recv.at[at],
+            device_id=device, device_id_type=MESH,
+        )
+
+    def start(self, at, src, dst, device):
+        copy = self.copy(at, src, dst, device)
+        copy.start()
+        return copy
+
+
+def add_into(count, target, *others):
+    def block(i, _):
+        total = target(i)[...].astype(F32)
+        for other in others:
+            total = total + other(i)[...].astype(F32)
+        target(i)[...] = total.astype(target(i).dtype)
+        return 0
+
+    lax.fori_loop(0, count, block, 0)
+
+
+class ExpertSums:
+    COPIES = 2 + OUTER - 1
+
+    def __init__(self, place, links, eg, own, part, x_rx, z_rx, out, local_sem):
+        self.p, self.links, self.out, self.sem = place, links, out, local_sem
+        self.eg, self.own, self.part, self.x_rx, self.z_rx = eg, own, part, x_rx, z_rx
+        self.count = eg.shape[0]
+        self.first = links.reserve(self.count * self.COPIES)
+
+    def load(self, j):
+        return pltpu.make_async_copy(self.eg.at[j, :, :, :, self.p.c], self.own.at[j % 2], self.sem.at[j % 2])
+
+    def core_copy(self, j):
+        return self.links.copy(
+            self.first + j * self.COPIES, self.eg.at[j, :, :, :, 1 - self.p.c], self.part.at[j], self.p.core
+        )
+
+    def across_copy(self, j):
+        return self.links.copy(
+            self.first + j * self.COPIES + 1, self.part.at[j, :, :, 1 - self.p.x], self.x_rx.at[j], self.p.across
+        )
+
+    def along_copy(self, j, k):
+        z = self.p.along[k]
+        return self.links.copy(
+            self.first + j * self.COPIES + 2 + k, self.part.at[j, :, z, self.p.x], self.z_rx.at[j, k], self.p.at_z(z)
+        )
+
+    def core(self, j):
+        if j < 2:
+            self.load(j).start()
+        self.core_copy(j).start()
+
+    def across(self, j):
+        p = self.p
+
+        def add(x):
+            add_into(
+                2 * OUTER,
+                lambda i: self.part.at[j, i // OUTER, i % OUTER, x],
+                lambda i: self.own.at[j % 2, i // OUTER, i % OUTER, x],
+            )
+
+        self.load(j).wait()
+        self.core_copy(j).wait()
+        add(1 - p.x)
+        self.across_copy(j).start()
+        add(p.x)
+        if j + 2 < self.count:
+            self.load(j + 2).start()
+
+    def along(self, j):
+        p = self.p
+        self.across_copy(j).wait()
+        add_into(
+            2 * OUTER,
+            lambda i: self.part.at[j, i // OUTER, i % OUTER, p.x],
+            lambda i: self.x_rx.at[j, i // OUTER, i % OUTER],
+        )
+        for k in range(OUTER - 1):
+            self.along_copy(j, k).start()
+
+    def finish(self, j):
+        p = self.p
+        for k in range(OUTER - 1):
+            self.along_copy(j, k).wait()
+        for half in range(2):
+            total = self.part[j, half, p.z, p.x].astype(F32)
+            for k in range(OUTER - 1):
+                total = total + self.z_rx[j, k, half].astype(F32)
+            self.out[j, half] = total
+
+
+class SharedSum:
+    COPIES = 2 * (3 + OUTER - 1)
+
+    def __init__(self, place, links, g, src, rx1, rx2, rx3, rx4, out):
+        self.p, self.links, self.out = place, links, out.at[g]
+        self.src, self.rx1, self.rx2, self.rx3, self.rx4 = src.at[g], rx1.at[g], rx2.at[g], rx3.at[g], rx4.at[g]
+        self.at = links.reserve(self.COPIES)
+
+    def start(self, *args):
+        copy = self.links.start(self.at, *args)
+        self.at += 1
+        return copy
+
+    def core(self):
+        p = self.p
+        self.c = self.start(self.src.at[1 - p.c], self.rx1, p.core)
+
+    def beside(self):
+        p = self.p
+        self.c.wait()
+        for y in (1 - p.y, p.y):
+            add_into(
+                2,
+                lambda i: self.src.at[p.c, y, i],
+                lambda i: self.rx1.at[y, i],
+            )
+            if y is not p.y:
+                self.c = self.start(self.src.at[p.c, y], self.rx2, p.beside)
+
+    def across(self):
+        p = self.p
+        self.c.wait()
+        for x in (1 - p.x, p.x):
+            add_into(1, lambda i: self.src.at[p.c, p.y, x], lambda i: self.rx2.at[x])
+            if x is not p.x:
+                self.c = self.start(self.src.at[p.c, p.y, x], self.rx3, p.across)
+
+    def along(self):
+        p = self.p
+        self.c.wait()
+        add_into(1, lambda i: self.src.at[p.c, p.y, p.x], lambda i: self.rx3)
+        self.cs = [
+            self.start(self.src.at[p.c, p.y, p.x, z], self.rx4.at[k], p.at_z(z)) for k, z in enumerate(p.along)
+        ]
+
+    def out_along(self):
+        p = self.p
+        for c in self.cs:
+            c.wait()
+        total = self.src[p.c, p.y, p.x, p.z].astype(F32)
+        for k in range(OUTER - 1):
+            total = total + self.rx4[k].astype(F32)
+        mine = self.out.at[p.c, p.y, p.x, p.z]
+        mine[...] = total.astype(BF)
+        self.cs = [self.start(mine, mine, p.at_z(z)) for z in p.along]
+
+    def out_across(self):
+        p = self.p
+        for c in self.cs:
+            c.wait()
+        mine = self.out.at[p.c, p.y, p.x]
+        self.c = self.start(mine, mine, p.across)
+
+    def out_beside(self):
+        p = self.p
+        self.c.wait()
+        mine = self.out.at[p.c, p.y]
+        self.c = self.start(mine, mine, p.beside)
+
+    def out_core(self):
+        p = self.p
+        self.c.wait()
+        mine = self.out.at[p.c]
+        self.c = self.start(mine, mine, p.core)
+
+    def finish(self):
+        self.c.wait()
+
+
+class SmallSum:
+    COPIES = 3 + OUTER - 1
+
+    def __init__(self, place, links, src, rx):
+        self.p, self.links, self.src, self.rx = place, links, src, rx
+        self.first = links.reserve(self.COPIES)
+
+    def step(self, k):
+        if k == 3:
+            return self.along()
+        device = (self.p.core, self.p.beside, self.p.across)[k]
+        if k:
+            self.c.wait()
+            self.src[k] = self.src[k - 1] + self.rx[k - 1]
+        self.c = self.links.start(self.first + k, self.src.at[k], self.rx.at[k], device)
+
+    def along(self):
+        self.c.wait()
+        self.src[3] = self.src[2] + self.rx[2]
+        self.cs = [
+            self.links.start(self.first + 3 + k, self.src.at[3], self.rx.at[3 + k], self.p.at_z(z))
+            for k, z in enumerate(self.p.along)
+        ]
+
+    def finish(self, out):
+        for c in self.cs:
+            c.wait()
+        total = self.src[3]
+        for k in range(OUTER - 1):
+            total = total + self.rx[3 + k]
+        out[...] = total
+
+
+ORDER = (
+    ("E", 1, "core"), ("d", 0, ""), ("run", 0, ""), ("d", 1, ""), ("E", 1, "across"), ("E", 0, "core"), ("d", 2, ""),
+    ("E", 3, "core"), ("run", 1, ""), ("d", 3, ""), ("run", 2, ""), ("run", 3, ""), ("E", 0, "across"),
+    ("run", 4, ""), ("E", 1, "along"), ("run", 5, ""), ("S", 0, "core"), ("run", 6, ""), ("run", 7, ""),
+    ("run", 8, ""), ("run", 9, ""), ("S", 0, "beside"), ("run", 10, ""), ("E", 3, "across"), ("run", 11, ""),
+    ("S", 1, "core"), ("E", 0, "along"), ("run", 12, ""), ("S", 1, "beside"), ("run", 13, ""), ("S", 2, "core"),
+    ("S", 0, "across"), ("E", 2, "core"), ("run", 14, ""), ("run", 15, ""), ("S", 2, "beside"), ("run", 16, ""),
+    ("S", 0, "along"), ("S", 1, "across"), ("run", 17, ""), ("run", 18, ""), ("S", 3, "core"), ("E", 0, "finish"),
+    ("S", 0, "out_along"), ("S", 1, "along"), ("S", 3, "beside"), ("S", 2, "across"), ("E", 1, "finish"),
+    ("run", 19, ""), ("few", 0, ""), ("S", 2, "along"), ("S", 0, "out_across"), ("E", 3, "along"), ("few", 1, ""),
+    ("y", 0, ""), ("S", 1, "out_along"), ("S", 3, "across"), ("S", 0, "out_beside"), ("few", 2, ""),
+    ("E", 2, "across"), ("S", 2, "out_along"), ("S", 3, "along"), ("few", 3, ""), ("S", 1, "out_across"),
+    ("S", 2, "out_across"), ("S", 3, "out_along"), ("few", 4, ""), ("S", 1, "out_beside"), ("S", 2, "out_beside"),
+    ("S", 3, "out_across"), ("E", 2, "along"), ("S", 1, "out_core"), ("S", 3, "out_beside"), ("S", 0, "out_core"),
+    ("E", 3, "finish"), ("S", 2, "out_core"), ("S", 3, "out_core"), ("E", 2, "finish"), ("S", 0, "finish"),
+    ("S", 2, "finish"), ("S", 1, "finish"), ("run", 20, ""), ("S", 3, "finish"),
+)
+
+LOADED = ("c", "x3", "cot", "d", "delta", "x2", "qkv", "o", "p", "wo", "wqkv", "x1", "wout", "gp", "u", "win", "y", "x0")
+
+
+def bwd_kernel(linked, *refs):
+    names = ["gains", "router_t", "routes", "wqkv", "wo", "win", "wout", "x0", "x1", "x2", "x3", "qkv1", "qkv2"]
+    names += ["o1", "o2", "p1", "p2", "u", "gp", "c", "cot", "d", "delta", "y"]
+    if linked:
+        names += ["d_send", "delta_send", "y_send", "eg"]
+    names += ["act_out", "gin_out", "shared_out", "small_out"]
+    if linked:
+        names += ["eg_out"]
+    names += ["v_" + n for n in LOADED] + ["gv", "a_scr", "dbr_scr", "dqkv_scr", "sem"]
+    if linked:
+        names += ["d_rx", "delta_rx", "y_rx", "own", "part", "x_rx", "z_rx", "src", "rx1", "rx2", "rx3", "rx4"]
+        names += ["small_src", "small_rx", "eg_sem", "send", "recv"]
+    r = dict(zip(names, refs, strict=True))
+    gains, gv, a_scr, dbr_scr, dqkv_scr = (r[n] for n in ("gains", "gv", "a_scr", "dbr_scr", "dqkv_scr"))
+    images = gv.shape[0]
     m = images * ROWS
     lo = lane_low(ROWS)
 
-    g0, g1, first, second = gate_rows(router_t[...], c[...].reshape(m, D), routes[...])
-    delta = delta_refs[0][0:1] + delta_refs[0][1:2]
-    for r in delta_refs[1:]:
-        delta = delta + (r[0:1] + r[1:2])
-    dl = g0 * g1 * delta
-    dlog = jnp.where(first, dl, jnp.where(second, -dl, 0.0)).astype(BF)
-    drouter[...] = dot(dlog, c[...].reshape(m, D))
-    gv[...] = t_dot(dlog, router_t[...]).reshape(images, ROWS, D)
-
-    def open_image(i, total):
-        y = y_refs[0][i].astype(F32)
-        dc = gv[i] + d_refs[0][i].astype(F32)
-        for k in range(1, groups):
-            y = y + y_refs[k][i].astype(F32)
-            dc = dc + d_refs[k][i].astype(F32)
-        act[i] = (x3[i] + y).astype(BF)
-        dx, by_gain = norm_back(dc, x3[i], gains[3:4])
-        gv[i] = cot[i].astype(F32) + dx
-        return total + jnp.sum(by_gain, axis=0, keepdims=True)
-
-    dgain[3:4] = lax.fori_loop(0, images, open_image, jnp.zeros((1, D), F32))
-
-    def attend_back(layer, gain_row, x, qkv, o, p, dqkv_out, dproj_out, last):
-        gain = gains[gain_row : gain_row + 1]
-
+    second = {"qkv": "qkv2", "o": "o2", "p": "p2"}
+    copies = {}
+
+    def fetch(name, source):
+        copies[name] = pltpu.make_async_copy(r[source], r["v_" + name], r["sem"].at[LOADED.index(name)])
+        copies[name].start()
+
+    def need(*wanted):
+        for name in wanted:
+            copies[name].wait()
+
+    if linked:
+        place = Place()
+        links = Links(r["send"], r["recv"])
+        place.meet([place.core, place.across, place.beside] + [place.at_z(z) for z in place.along])
+        delta_copy = links.start(links.reserve(1), r["delta_send"], r["delta_rx"], place.beside)
+        d_first = links.reserve(images)
+
+        def d_copy(i):
+            return links.copy(d_first + i, r["d_send"].at[i], r["d_rx"].at[i], place.beside)
+
+        experts = ExpertSums(
+            place, links, r["eg"], r["own"], r["part"], r["x_rx"], r["z_rx"], r["eg_out"], r["eg_sem"]
+        )
+        y_copy = links.copy(links.reserve(1), r["y_send"], r["y_rx"], place.beside)
+        sums = [
+            SharedSum(place, links, g, r["src"], r["rx1"], r["rx2"], r["rx3"], r["rx4"], r["shared_out"])
+            for g in range(4)
+        ]
+        few = SmallSum(place, links, r["small_src"], r["small_rx"])
+        shared, small = r["src"], r["small_src"].at[0]
+        small[...] = jnp.zeros(small.shape, F32)
+    else:
+        shared, small = r["shared_out"], r["small_out"]
+    for name in LOADED:
+        fetch(name, second.get(name, name))
+
+    def keep(block, value):
+        if linked:
+            shared[block // 4, (block % 4) // 2, block % 2] = value.astype(BF).reshape(2, OUTER, SHARE, D)
+        else:
+            shared[block] = value.astype(BF)
+
+    def router():
+        need("c", "delta")
+        c_all = r["v_c"][...].reshape(m, D)
+        g0, g1, first, other = gate_rows(r["router_t"][...], c_all, r["routes"][...])
+        delta = r["v_delta"][0:1] + r["v_delta"][1:2]
+        if linked:
+            delta_copy.wait()
+            delta = delta + (r["delta_rx"][0:1] + r["delta_rx"][1:2])
+        dl = g0 * g1 * delta
+        dlog = jnp.where(first, dl, jnp.where(other, -dl, 0.0)).astype(BF)
+        small[4 : 4 + dlog.shape[0]] = dot(dlog, c_all)
+        small[0:4] = jnp.zeros((4, D), F32)
+        gv[...] = t_dot(dlog, r["router_t"][...]).reshape(images, ROWS, D)
+        need("x3", "cot", "d")
+
+    def add_gain(row, by_gain):
+        small[row : row + 1] += jnp.sum(by_gain, axis=0, keepdims=True)
+
+    def first(i):
+        dc = gv[i] + r["v_d"][i].astype(F32)
+        if linked:
+            d_copy(i).wait()
+            dc = dc + r["d_rx"][i].astype(F32)
+        dx, by_gain = norm_back(dc, r["v_x3"][i], gains[3:4])
+        gv[i] = r["v_cot"][i].astype(F32) + dx
+        add_gain(3, by_gain)
+        if i == 0:
+            need("x2", "qkv", "o", "p", "wo")
+        attend_image(i, 1, gains[2:3], r["v_x2"])
+
+    def attend_image(i, layer, gain, x):
+        qkv, o, p = r["v_qkv"], r["v_o"], r["v_p"]
+        a_scr[i] = (norm_parts(x[i].astype(F32))[0] * gain).astype(BF)
+        dbr = gv[i].astype(BF)
+        dbr_scr[i] = dbr
+        do = dot_t(dbr, r["v_wo"][layer]).astype(BF)
+        dod = do.astype(F32) * o[i].astype(F32)
+        for pair in range(HEADS // 2):
+            at = 128 * pair
+            q = qkv[i, :, at : at + 128] * BF(0.125)
+            k = qkv[i, :, D + at : D + at + 128]
+            w = qkv[i, :, 2 * D + at : 2 * D + at + 128]
+            dqs, dk, dw = [], 0.0, 0.0
+            for h in range(2):
+                mask = lo if h == 0 else ~lo
+                dom = jnp.where(mask, do[:, at : at + 128], BF(0))
+                inner = jnp.sum(jnp.where(mask, dod[:, at : at + 128], 0.0), axis=-1, keepdims=True)
+                ph = p[i, 2 * pair + h]
+                ds = (ph.astype(F32) * (dot_t(dom, w) - inner)).astype(BF)
+                dw = dw + t_dot(ph, dom)
+                dqs.append(dot(ds, k))
+                dk = dk + t_dot(ds, jnp.where(mask, q, BF(0)))
+            dqkv_scr[i, :, at : at + 128] = (jnp.where(lo, dqs[0], dqs[1]) * 0.125).astype(BF)
+            dqkv_scr[i, :, D + at : D + at + 128] = dk.astype(BF)
+            dqkv_scr[i, :, 2 * D + at : 2 * D + at + 128] = dw.astype(BF)
+
+    def attend_weights(block):
+        a_all = a_scr[...].reshape(m, D)
+        for f in range(3):
+            keep(block + f, t_dot(a_all, dqkv_scr[:, :, f * D : f * D + D].reshape(m, D)))
+        keep(block + 3, t_dot(r["v_o"][...].reshape(m, D), dbr_scr[...].reshape(m, D)))
+
+    def close(x, layer, row, out):
         def image(i, _):
-            a_scr[i] = (norm_parts(x[i].astype(F32))[0] * gain).astype(BF)
-            dbr = gv[i].astype(BF)
-            dbr_scr[i] = dbr
-            do = dot_t(dbr, wo[layer])
-            dod = do.astype(BF).astype(F32) * o[i].astype(F32)
-            do = do.astype(BF)
-            for pair in range(HEADS // 2):
-                at = 128 * pair
-                q = qkv[i, :, at : at + 128] * BF(0.125)
-                k = qkv[i, :, D + at : D + at + 128]
-                w = qkv[i, :, 2 * D + at : 2 * D + at + 128]
-                dqs, dk, dw = [], 0.0, 0.0
-                for h in range(2):
-                    mask = lo if h == 0 else ~lo
-                    dom = jnp.where(mask, do[:, at : at + 128], BF(0))
-                    inner = jnp.sum(jnp.where(mask, dod[:, at : at + 128], 0.0), axis=-1, keepdims=True)
-                    ph = p[i, 2 * pair + h]
-                    ds = (ph.astype(F32) * (dot_t(dom, w) - inner)).astype(BF)
-                    dw = dw + t_dot(ph, dom)
-                    dqs.append(dot(ds, k))
-                    dk = dk + t_dot(ds, jnp.where(mask, q, BF(0)))
-                big[i, :, at : at + 128] = (jnp.where(lo, dqs[0], dqs[1]) * 0.125).astype(BF)
-                big[i, :, D + at : D + at + 128] = dk.astype(BF)
-                big[i, :, 2 * D + at : 2 * D + at + 128] = dw.astype(BF)
+            da = dot_t(dqkv_scr[i], r["v_wqkv"][layer])
+            dx, by_gain = norm_back(da, x[i].astype(F32), gains[row : row + 1])
+            out[i] = gv[i] + dx
+            add_gain(row, by_gain)
             return 0
 
         lax.fori_loop(0, images, image, 0)
-        dproj_out[...] = t_dot(o[...].reshape(m, D), dbr_scr[...].reshape(m, D)).astype(BF)
-        a_all = a_scr[...].reshape(m, D)
-        for f in range(0, 3 * D, D):
-            dqkv_out[:, f : f + D] = t_dot(a_all, big[:, :, f : f + D].reshape(m, D)).astype(BF)
-
-        def close(i, total):
-            da = dot_t(big[i, :, 0 : 3 * D], wqkv[layer])
-            dx, by_gain = norm_back(da, x[i].astype(F32), gain)
-            new = gv[i] + dx
-            if last:
-                gin[i] = new
-            else:
-                gv[i] = new
-            return total + jnp.sum(by_gain, axis=0, keepdims=True)
-
-        dgain[gain_row : gain_row + 1] = lax.fori_loop(0, images, close, jnp.zeros((1, D), F32))
-
-    attend_back(1, 2, x2, qkv2, o2, p2, dqkv_b, dproj_b, False)
-
-    def mlp_image(i, _):
-        a_scr[i] = (norm_parts(x1[i])[0] * gains[1:2]).astype(BF)
+
+    def first_close():
+        for name in ("qkv", "o", "p"):
+            fetch(name, name + "1")
+        need("wqkv")
+        close(r["v_x2"], 1, 2, gv)
+        need("x1", "wout", "gp", "u", "win")
+
+    gp = r["v_gp"]
+
+    def mlp(i):
+        a_scr[i] = (norm_parts(r["v_x1"][i])[0] * gains[1:2]).astype(BF)
         dm = gv[i].astype(BF)
         dbr_scr[i] = dm
         for f in range(0, FF, 512):
-            big[i, :, f : f + 512] = (dot_t(dm, wout[f : f + 512]) * gp[i, :, f : f + 512].astype(F32)).astype(BF)
-        return 0
-
-    lax.fori_loop(0, images, mlp_image, 0)
-    dm_all = dbr_scr[...].reshape(m, D)
-    b_all = a_scr[...].reshape(m, D)
-    for f in range(0, FF, 512):
-        dwout[f : f + 512] = t_dot(u[:, :, f : f + 512].reshape(m, 512), dm_all).astype(BF)
-        dwin[:, f : f + 512] = t_dot(b_all, big[:, :, f : f + 512].reshape(m, 512)).astype(BF)
-
-    def mlp_close(i, total):
-        db = dot_t(big[i], win[...])
-        dx, by_gain = norm_back(db, x1[i], gains[1:2])
-        gv[i] = gv[i] + dx
-        return total + jnp.sum(by_gain, axis=0, keepdims=True)
-
-    dgain[1:2] = lax.fori_loop(0, images, mlp_close, jnp.zeros((1, D), F32))
-
-    attend_back(0, 0, x0, qkv1, o1, p1, dqkv_a, dproj_a, True)
-
-
-def dense_backward(weights, saved, cot, routes, ys, ds, deltas):
-    groups = len(ys)
-    images = saved[0].shape[0]
-    experts = weights[-1].shape[0]
-    ins = list(weights) + list(saved) + [cot, routes] + list(ys) + list(ds) + list(deltas)
+            du = dot_t(dm, r["v_wout"][f : f + 512])
+            gp[i, :, f : f + 512] = (du * gp[i, :, f : f + 512].astype(F32)).astype(BF)
+
+    def mlp_out_weights():
+        dm_all = dbr_scr[...].reshape(m, D)
+        for f in range(4):
+            keep(4 + f, t_dot(r["v_u"][:, :, f * D : f * D + D].reshape(m, D), dm_all))
+
+    def mlp_in_weights():
+        b_all = a_scr[...].reshape(m, D)
+        for f in range(4):
+            keep(8 + f, t_dot(b_all, gp[:, :, f * D : f * D + D].reshape(m, D)))
+
+    def mlp_close():
+        def image(i, _):
+            db = dot_t(gp[i], r["v_win"][...])
+            dx, by_gain = norm_back(db, r["v_x1"][i], gains[1:2])
+            gv[i] = gv[i] + dx
+            add_gain(1, by_gain)
+            return 0
+
+        lax.fori_loop(0, images, image, 0)
+        need("x0", "qkv", "o", "p")
+
+    def last(i):
+        attend_image(i, 0, gains[0:1], r["v_x0"])
+
+    def last_close():
+        close(r["v_x0"], 0, 0, r["gin_out"])
+
+    def act():
+        need("y")
+        if linked:
+            y_copy.wait()
+        for i in range(images):
+            x4 = r["v_x3"][i] + r["v_y"][i].astype(F32)
+            if linked:
+                x4 = x4 + r["y_rx"][i].astype(F32)
+            r["act_out"][i] = x4.astype(BF)
+
+    compute = [router] + [functools.partial(first, i) for i in range(images)]
+    compute += [lambda: attend_weights(0), first_close] + [functools.partial(mlp, i) for i in range(images)]
+    compute += [mlp_out_weights, mlp_in_weights, mlp_close] + [functools.partial(last, i) for i in range(images)]
+    compute += [lambda: attend_weights(12), last_close, act]
+    if not linked:
+        for step in compute:
+            step()
+        return
+    done = 0
+    for kind, at, what in ORDER:
+        if kind == "run":
+            compute[done]()
+            done += 1
+        elif kind == "d":
+            d_copy(at).start()
+        elif kind == "y":
+            y_copy.start()
+        elif kind == "few" and at < 4:
+            few.step(at)
+        elif kind == "few":
+            few.finish(r["small_out"])
+        elif kind == "E":
+            getattr(experts, what)(at)
+        else:
+            getattr(sums[at], what)()
+
+
+def dense_backward(weights, router_t, routes, saved, cot, d, delta, y, sent=None):
+    gains, wqkv, wo, win, wout = weights
+    x0, x1, x2, x3, qkv1, qkv2, o1, o2, p1, p2, u, gp, c = saved
+    images = x0.shape[0]
+    linked = sent is not None
+    small_rows = 16 if linked else 4 + router_t.shape[0]
+    ins = [gains, router_t, routes, wqkv, wo, win, wout, *saved, cot, d, delta, y] + (list(sent) if linked else [])
     outs = [
         jax.ShapeDtypeStruct((images, ROWS, D), BF),
         jax.ShapeDtypeStruct((images, ROWS, D), F32),
-        jax.ShapeDtypeStruct((D, 3 * D), BF),
-        jax.ShapeDtypeStruct((D, 3 * D), BF),
-        jax.ShapeDtypeStruct((D, D), BF),
-        jax.ShapeDtypeStruct((D, D), BF),
-        jax.ShapeDtypeStruct((4, D), F32),
-        jax.ShapeDtypeStruct((D, FF), BF),
-        jax.ShapeDtypeStruct((FF, D), BF),
-        jax.ShapeDtypeStruct((experts, D), F32),
+        jax.ShapeDtypeStruct((4, 2, 2, 2, OUTER, SHARE, D) if linked else (16, D, D), BF),
+        jax.ShapeDtypeStruct((small_rows, D), F32),
     ]
+    vm = pltpu.VMEM
+    loaded = dict(
+        c=c, x3=x3, cot=cot, d=d, delta=delta, x2=x2, qkv=qkv1, o=o1, p=p1, wo=wo, wqkv=wqkv, x1=x1, wout=wout,
+        gp=gp, u=u, win=win, y=y, x0=x0,
+    )
+    scratch = [vm(loaded[name].shape, loaded[name].dtype) for name in LOADED]
+    scratch += [vm((images, ROWS, D), F32), vm((images, ROWS, D), BF), vm((images, ROWS, D), BF)]
+    scratch += [vm((images, ROWS, 3 * D), BF), pltpu.SemaphoreType.DMA((len(LOADED),))]
+    params = dict(vmem_limit_bytes=62 << 20)
+    if linked:
+        eg = sent[-1]
+        local, share = eg.shape[0], eg.shape[-2]
+        outs.append(jax.ShapeDtypeStruct((local, 2, share, D), F32))
+        copies = 2 + images + local * ExpertSums.COPIES + 4 * SharedSum.COPIES + SmallSum.COPIES
+        scratch += [vm(d.shape, BF), vm(delta.shape, F32), vm(y.shape, BF)]
+        scratch += [
+            vm((2, 2, OUTER, 2, share, D), BF),
+            vm((local, 2, OUTER, 2, share, D), BF),
+            vm((local, 2, OUTER, share, D), BF),
+            vm((local, OUTER - 1, 2, share, D), BF),
+            vm((4, 2, 2, 2, OUTER, SHARE, D), BF),
+            vm((4, 2, 2, OUTER, SHARE, D), BF),
+            vm((4, 2, OUTER, SHARE, D), BF),
+            vm((4, OUTER, SHARE, D), BF),
+            vm((4, OUTER - 1, SHARE, D), BF),
+            vm((4, small_rows, D), F32),
+            vm((OUTER + 2, small_rows, D), F32),
+            pltpu.SemaphoreType.DMA((2,)),
+            pltpu.SemaphoreType.DMA((copies,)),
+            pltpu.SemaphoreType.DMA((copies,)),
+        ]
+        params.update(collective_id=1, has_side_effects=True)
     return pl.pallas_call(
-        functools.partial(bwd_kernel, groups, len(ins)),
+        functools.partial(bwd_kernel, linked),
         out_shape=outs,
-        in_specs=[VMEM] * len(ins),
+        in_specs=[VMEM] * 3 + [pl.BlockSpec(memory_space=pl.ANY)] * (len(ins) - 3),
         out_specs=[VMEM] * len(outs),
-        scratch_shapes=[
-            pltpu.VMEM((images, ROWS, D), F32),
-            pltpu.VMEM((images, ROWS, D), BF),
-            pltpu.VMEM((images, ROWS, D), BF),
-            pltpu.VMEM((images, ROWS, FF), BF),
-        ],
-        compiler_params=pltpu.CompilerParams(vmem_limit_bytes=60 << 20),
+        scratch_shapes=scratch,
+        compiler_params=pltpu.CompilerParams(**params),
         name="dense_backward",
     )(*ins)
 
 
+def finish_kernel(
+    act, gin, shared, small, eg, act_out, gin_out, qkv_out, proj_out, gain_out, mlp_in_out, mlp_out_out, router_out,
+    in_out, out_out, v_shared, v_wide, v_gin, v_act, in_sem, out_sem,
+):
+    images = act.shape[0]
+    blocks = v_shared.shape[0]
+    targets = {3: proj_out.at[1], 15: proj_out.at[0]}
+    for f in range(3):
+        targets[f] = qkv_out.at[1, :, pl.ds(f * D, D)]
+        targets[12 + f] = qkv_out.at[0, :, pl.ds(f * D, D)]
+    for f in range(4):
+        targets[4 + f] = mlp_out_out.at[pl.ds(f * D, D)]
+        targets[8 + f] = mlp_in_out.at[:, pl.ds(f * D, D)]
+
+    def load(b):
+        return pltpu.make_async_copy(shared.at[b], v_shared.at[b], in_sem.at[b])
+
+    def store(b):
+        return pltpu.make_async_copy(v_wide.at[b], targets[b], out_sem.at[b])
+
+    load_gin = pltpu.make_async_copy(gin, v_gin, in_sem.at[blocks])
+    load_act = pltpu.make_async_copy(act, v_act, in_sem.at[blocks + 1])
+    for b in range(blocks):
+        load(b).start()
+    load_gin.start()
+    load_act.start()
+    gain_out[...] = small[0:4]
+    router_out[...] = small[4 : 4 + router_out.shape[0]]
+    for e in range(eg.shape[0]):
+        in_out[e] = eg[e, 0]
+        out_out[e] = eg[e, 1]
+    for b in range(blocks):
+        load(b).wait()
+        v_wide[b] = v_shared[b].astype(F32)
+        store(b).start()
+    load_gin.wait()
+    load_act.wait()
+    for i in range(images):
+        gin_out[i * PATCHES : (i + 1) * PATCHES] = v_act[i, 0:PATCHES].astype(F32)
+    act_out[...] = gin_out[...].astype(BF)
+    for i in range(images):
+        gin_out[i * PATCHES : (i + 1) * PATCHES] = v_gin[i, 0:PATCHES]
+    for b in range(blocks):
+        store(b).wait()
+
+
+def finish(act, gin, shared, small, eg, experts):
+    images, local, share = act.shape[0], eg.shape[0], eg.shape[2]
+    row_count = images * PATCHES
+    outs = [
+        jax.ShapeDtypeStruct((row_count, D), BF),
+        jax.ShapeDtypeStruct((row_count, D), F32),
+        jax.ShapeDtypeStruct((2, D, 3 * D), F32),
+        jax.ShapeDtypeStruct((2, D, D), F32),
+        jax.ShapeDtypeStruct((4, D), F32),
+        jax.ShapeDtypeStruct((D, FF), F32),
+        jax.ShapeDtypeStruct((FF, D), F32),
+        jax.ShapeDtypeStruct((experts, D), F32),
+        jax.ShapeDtypeStruct((local, share, D), F32),
+        jax.ShapeDtypeStruct((local, share, D), F32),
+    ]
+    far = pl.BlockSpec(memory_space=pl.ANY)
+    return pl.pallas_call(
+        finish_kernel,
+        out_shape=outs,
+        in_specs=[far, far, far, VMEM, VMEM],
+        out_specs=[VMEM, VMEM, far, far, VMEM, far, far, VMEM, VMEM, VMEM],
+        scratch_shapes=[
+            pltpu.VMEM(shared.shape, BF),
+            pltpu.VMEM(shared.shape, F32),
+            pltpu.VMEM(gin.shape, F32),
+            pltpu.VMEM(act.shape, BF),
+            pltpu.SemaphoreType.DMA((shared.shape[0] + 2,)),
+            pltpu.SemaphoreType.DMA((shared.shape[0],)),
+        ],
+        compiler_params=pltpu.CompilerParams(vmem_limit_bytes=62 << 20),
+        name="finish",
+    )(act, gin, shared, small, eg)
+
+
 def from_peer(array, groups, shift):
     return lax.ppermute(array, "exp", [(i, (i + shift) % groups) for i in range(groups)])
 
 
-def pad_images(rows, value=0):
+def pad_images(rows):
     rows = rows.reshape(-1, PATCHES, rows.shape[-1])
-    return jnp.pad(rows, ((0, 0), (0, ROWS - PATCHES), (0, 0)), constant_values=value)
+    return jnp.pad(rows, ((0, 0), (0, ROWS - PATCHES), (0, 0)))
 
 
 def shards(
@@ -471,8 +943,9 @@
     images = row_count // PATCHES
     n_tok = images * ROWS
     x0, cot = pad_images(tokens), pad_images(cotangent)
-    routes_t = pad_images(routes, -1).reshape(n_tok, choices).T
-    routes_t = jnp.pad(routes_t, ((0, 8 - choices), (0, 0)), constant_values=-1)
+    routes_t = routes.T.reshape(choices, images, PATCHES)
+    routes_t = jnp.pad(routes_t, ((0, 8 - choices), (0, 0), (0, ROWS - PATCHES)), constant_values=-1)
+    routes_t = routes_t.reshape(8, n_tok)
     router_t = router.T
     flat = cot.reshape(n_tok, D)
     gs = [flat] + [from_peer(flat, groups, k) for k in range(1, groups)]
@@ -482,36 +955,41 @@
     )
     c_flat = c.reshape(n_tok, D)
     cs = [c_flat] + [from_peer(c_flat, groups, k) for k in range(1, groups)]
-    eg, ys, ds, deltas = experts_all(cs, gs, rs, router_t, experts_in, experts_out, local * capacity * groups)
-
-    def back(parts):
-        return [parts[0]] + [from_peer(parts[k], groups, groups - k) for k in range(1, groups)]
-
-    ds, deltas, ys = back(ds), back(deltas), back(ys)
-    ys = [y.reshape(images, ROWS, D) for y in ys]
-    ds = [d.reshape(images, ROWS, D) for d in ds]
     rep = lax.axis_size("rep")
-    eg = lax.psum_scatter(eg, "rep", scatter_dimension=2, tiled=True)
-    act, gin, dqkv_a, dqkv_b, dproj_a, dproj_b, dgain, dwin, dwout, drouter = dense_backward(
-        (norm_gains, attn_qkv, attn_out, mlp_in, mlp_out, router_t),
-        (x0, x1, x2, x3, qkv1, qkv2, o1, o2, p1, p2, u, gp, c),
-        cot, routes_t, ys, ds, deltas,
+    known = (rep, groups, local) == (16, 2, 4)
+    owners = (OUTER, 2, 2) if known else (rep,)
+    eg, ys, ds, deltas = experts_all(
+        cs, gs, rs, router_t, experts_in, experts_out, local * capacity * groups, owners
     )
-    dqkv_a, dqkv_b, dproj_a, dproj_b, dwin, dwout, dgain, drouter = lax.psum(
-        (dqkv_a, dqkv_b, dproj_a, dproj_b, dwin, dwout, dgain, drouter), ("rep", "exp")
-    )
-    return (
-        act[:, :PATCHES].reshape(row_count, D),
-        gin[:, :PATCHES].reshape(row_count, D),
-        jnp.stack([dqkv_a, dqkv_b]).astype(F32),
-        jnp.stack([dproj_a, dproj_b]).astype(F32),
-        dgain,
-        dwin.astype(F32),
-        dwout.astype(F32),
-        drouter.T,
-        jnp.swapaxes(eg[:, 0], 1, 2).astype(F32),
-        eg[:, 1].astype(F32),
-    )
+
+    weights = (norm_gains, attn_qkv, attn_out, mlp_in, mlp_out)
+    saved = (x0, x1, x2, x3, qkv1, qkv2, o1, o2, p1, p2, u, gp, c)
+    by_image = (images, ROWS, D)
+    experts = router_t.shape[0]
+    if known:
+        sent = (ds[1].reshape(by_image), deltas[1], ys[1].reshape(by_image), eg)
+        act, gin, shared, small, eg = dense_backward(
+            weights, router_t, routes_t, saved, cot, ds[0].reshape(by_image), deltas[0], ys[0].reshape(by_image), sent
+        )
+        shared = shared.reshape(16, D, D)
+    else:
+
+        def back(parts):
+            total = parts[0].astype(F32)
+            for k in range(1, groups):
+                total = total + from_peer(parts[k], groups, groups - k).astype(F32)
+            return total
+
+        d, delta, y = back(ds).astype(BF), back(deltas), back(ys).astype(BF)
+        act, gin, shared, small = dense_backward(
+            weights, router_t, routes_t, saved, cot, d.reshape(by_image), delta, y.reshape(by_image)
+        )
+        eg = lax.psum_scatter(eg, "rep", scatter_dimension=2, tiled=True).reshape(local, 2, FF // rep, D).astype(F32)
+        shared, small = lax.psum((shared, small), ("rep", "exp"))
+    outs = list(finish(act, gin, shared, small, eg, experts))
+    outs[7] = outs[7].T
+    outs[8] = jnp.swapaxes(outs[8], 1, 2)
+    return tuple(outs)
 
 
 def solution(mesh):

time: 400 us -> 256 us (0.64); the launches traced: 405 us -> 252 us
  waiting for transfers between devices: 178 us -> 14.4 us
  Pallas kernels: 119 us -> 228 us
  blocking collectives: 55 us -> 0 us
  between operations: 15.7 us -> 1.19 us
  starting transfers between devices: 18.8 us -> 5.18 us
  other arithmetic: 9.88 us -> 0 us
  local copies, waits for them, and re-layouts: 8.3 us -> 3.66 us
    psum x1 -> x0, waiting for transfers between devices: 142 us -> none  [shards(): lax.psum((dqkv_a, dqkv_b, dproj_a, dproj_b, dwin, dwout, dgain, drouter),...]
    pallas_call x1 -> x2, Pallas kernels: 42 us -> 131 us  [the longest x1 122 us: dense_backward(): pl.pallas_call(functools.partial(bwd_kernel, linked), out_shape=outs, in_...]
    psum x1 -> x0, blocking collectives: 55 us -> none  [shards(): lax.psum((dqkv_a, dqkv_b, dproj_a, dproj_b, dwin, dwout, dgain, drouter),...]
    ppermute x6 -> x3, waiting for transfers between devices: 35.4 us -> 14.4 us  [from_peer(): lax.ppermute(array, 'exp', [(i, (i + shift) % groups) for i in range(grou...]
    pallas_call x1, Pallas kernels: 53.9 us -> 73.4 us  [experts_all(): pl.pallas_call(functools.partial(experts_kernel, groups, local, 'exp'), g...]
    ppermute x6 -> x3, starting transfers between devices: 18.7 us -> 5.18 us  [from_peer(): lax.ppermute(array, 'exp', [(i, (i + shift) % groups) for i in range(grou...]
    convert_element_type x5 -> x0, other arithmetic: 9.88 us -> none  [the longest x1 3.06 us: shards(): dwin.astype(F32)]
  transfers between devices with their start and end apart: 8 -> 3, of which waited for: 3 -> 1; matrix products, arithmetic and copies ran while one was open for 3% -> 0% of each run, Pallas kernels for 6% -> 9%
where the time goes in v3:
time: 256 us; the launch traced here: 252 us
  Pallas kernels  228 us (89%)
  waiting for transfers between devices  14.4 us (6%)
  starting transfers between devices  5.18 us (2%)
  local copies, waits for them, and re-layouts  3.66 us (1%)
    pallas_call x1, Pallas kernels, dense_backward(): pl.pallas_call(functools.partial(bwd_kernel, linked), out_shape=outs, in_...  122 us
    pallas_call x1, Pallas kernels, experts_all(): pl.pallas_call(functools.partial(experts_kernel, groups, local, 'exp'), g...  73.4 us
    pallas_call x1, Pallas kernels, dense_forward(): pl.pallas_call(fwd_kernel, grid=(n // ib,), out_shape=outs, in_specs=[blo...  23.4 us
    ppermute x3, waiting for transfers between devices, from_peer(): lax.ppermute(array, 'exp', [(i, (i + shift) % groups) for i in range(grou...  14.4 us
    pallas_call x1, Pallas kernels, finish(): pl.pallas_call(finish_kernel, out_shape=outs, in_specs=[far, far, far, VM...  8.73 us
    ppermute x3, starting transfers between devices, from_peer(): lax.ppermute(array, 'exp', [(i, (i + shift) % groups) for i in range(grou...  5.18 us
  transfers between devices with their start and end apart: 3, of which 1 were waited for; matrix products, arithmetic and copies ran while one was open for 0% of the time, Pallas kernels for 9%

profile of v3, /device:TPU:0, one launch (start us, length us, event | category | flops | bytes accessed | tf_op | source)
XLA Modules:
  0.0 252.0 jit_solution(9038232884283616091)
XLA Ops:
  0.6 0.0 copy-start.3
  0.7 1.3 reshape.56
  2.0 0.1 pad.13.refs_20_
  2.0 0.0 copy-start
  2.0 3.0 %collective-permute-start.1 = (bf16[832,384]{1,0:T(8,128)(2,1)S(1)}, bf16[832,384]{1,0:T(8,128)(2,1)S(1)}, u32[]{:S(2)}, u32[]{:S(2)}) collective-permute-start(bf16[832,384]{1,0:T(8,128)(2,1)S(1)} %bitcast.11), channel_id=1, source_target_pairs={{0,1},{1,0},{2,3},{3,2},{4,5},{5,4},{6,7},{7,6},{8,9},{9,8},{10,11... | collective-permute-start | bytes 1916936 | tf_op jit(solution)/shard_map/ppermute | solution.py:927
  5.1 0.0 copy-done.3
  5.1 0.2 reshape.55
  5.2 0.9 pad.12.x_ref.refs_7_
  6.1 0.0 copy-start.6
  6.1 23.4 %dense_forward.1 = (f32[4,208,384]{2,1,0:T(8,128)}, f32[4,208,384]{2,1,0:T(8,128)}, f32[4,208,384]{2,1,0:T(8,128)}, bf16[4,208,1152]{2,1,0:T(8,128)(2,1)}, bf16[...) custom-call(bf16[4,208,384]{2,1,0:T(8,128)(2,1)} %pad.12.x_ref.refs_, ...), custom_call_target="tpu_custom_call" | custom-call | tf_op jit(solution)/shard_map/dense_forward/pallas_call | solution.py:123
  29.6 0.0 copy-done
  29.6 0.1 collective-permute-start
  29.7 0.0 copy-done.6
  29.7 0.1 reshape.53
  29.8 0.1 reshape.54.refs_4_.refs_2_
  29.9 0.0 copy-start.4
  29.9 2.1 collective-permute-start.2
  31.9 14.4 %collective-permute-done.2.refs_5_ = s32[8,832]{1,0:T(8,128)S(1)} collective-permute-done((s32[8,832]{1,0:T(8,128)S(1)}, s32[8,832]{1,0:T(8,128)S(1)}, u32[]{:S(2)}, u32[]{:S(2)}) %collective-permute-start.2) | collective-permute-done | bytes 26656 | tf_op jit(solution)/shard_map/ppermute | solution.py:927
  46.3 0.0 copy-start.5
  46.3 0.0 collective-permute-done.1.refs_3_
  46.3 0.0 copy-start.1
  46.3 0.0 collective-permute-done.refs_1_
  46.3 0.0 copy-start.2
  46.3 0.0 copy-done.4
  46.4 0.6 copy-done.5
  46.9 0.2 copy-done.1
  47.2 0.2 copy-done.2
  47.4 73.4 %experts.1 = (bf16[4,2,4,2,2,96,384]{6,5,4,3,2,1,0:T(8,128)(2,1)}, bf16[832,384]{1,0:T(8,128)(2,1)}, bf16[832,384]{1,0:T(8,128)(2,1)}, bf16[832,384]{1,0:T(8,128...) custom-call(bf16[832,384]{1,0:T(8,128)(2,1)} %bitcast.15, bf16[832,384]{1,0:T(8,128)(2,1)} %copy-done.2, ...), custom_call_target="tpu_custom_call" | custom-call | tf_op jit(solution)/shard_map/experts/pallas_call | solution.py:288
  120.8 122.0 %dense_backward.1 = (bf16[4,208,384]{2,1,0:T(8,128)(2,1)}, f32[4,208,384]{2,1,0:T(8,128)}, bf16[4,2,2,2,4,48,384]{6,5,4,3,2,1,0:T(8,128)(2,1)}, f32[16,384]{1,0:T(8,128)}, f32[4,2,96,384]{3,2,1,0:T(8,128)}) custom-call(f32[4,384]{1,0:T(4,128)} %refs_0_.1, bf16[8,384]{1,0:T(8,128)(2,1)} %bitcast.21, s32[8,832]{1,0:T(8,128)} %copy-done.4, ...), custom_call_target="tpu_custom_call" | custom-call | tf_op jit(solution)/shard_map/dense_backward/pallas_call | solution.py:835
  242.8 8.7 %finish.1 = (bf16[788,384]{1,0:T(8,128)(2,1)}, f32[788,384]{1,0:T(8,128)}, f32[2,384,1152]{2,1,0:T(8,128)}, f32[2,384,384]{2,1,0:T(8,128)}, f32[4,384]{1,0:T(4,1...) custom-call(bf16[4,208,384]{2,1,0:T(8,128)(2,1)} %get-tuple-element., ...), custom_call_target="tpu_custom_call" | custom-call | tf_op jit(solution)/shard_map/finish/pallas_call | solution.py:908
  (1 shorter events, 0.0 us)
Async XLA Ops:
  0.6 4.4 %copy-start.3 = (bf16[788,384]{1,0:T(8,128)(2,1)S(1)}, bf16[788,384]{1,0:T(8,128)(2,1)}, u32[]{:S(2)}) copy-start(bf16[788,384]{1,0:T(8,128)(2,1)} %param.11) | copy-start | bytes 1815556
  2.0 27.6 %copy-start = (bf16[4,208,384]{2,1,0:T(8,128)(2,1)}, bf16[4,208,384]{2,1,0:T(8,128)(2,1)S(1)}, u32[]{:S(2)}) copy-start(bf16[4,208,384]{2,1,0:T(8,128)(2,1)S(1)} %pad.13.refs_20_) | copy-start | bytes 1916932
  2.0 44.3 %collective-permute-start.1 = (bf16[832,384]{1,0:T(8,128)(2,1)S(1)}, bf16[832,384]{1,0:T(8,128)(2,1)S(1)}, u32[]{:S(2)}, u32[]{:S(2)}) collective-permute-start(bf16[832,384]{1,0:T(8,128)(2,1)S(1)} %bitcast.11), channel_id=1, source_target_pairs={{0,1},{1,0},{2,3},{3,2},{4,5},{5,4},{6,7},{7,6},{8,9},{9,8},{10,11... | collective-permute-start | bytes 1916936 | tf_op jit(solution)/shard_map/ppermute | solution.py:927
  6.1 23.5 %copy-start.6 = (s32[788,2]{0,1:T(2,128)S(1)}, s32[788,2]{0,1:T(2,128)}, u32[]{:S(2)}) copy-start(s32[788,2]{0,1:T(2,128)} %param.12) | copy-start | bytes 18916
  29.6 16.7 %collective-permute-start = (bf16[832,384]{1,0:T(8,128)(2,1)}, bf16[832,384]{1,0:T(8,128)(2,1)S(1)}, u32[]{:S(2)}, u32[]{:S(2)}) collective-permute-start(bf16[832,384]{1,0:T(8,128)(2,1)} %bitcast.14), channel_id=1, source_target_pairs={{0,1},{1,0},{2,3},{3,2},{4,5},{5,4},{6,7},{7,6},{8,9},{9,8},{10,11... | collective-permute-start | bytes 1916936 | tf_op jit(solution)/shard_map/ppermute | solution.py:927
  29.9 16.5 %copy-start.4 = (s32[8,832]{1,0:T(8,128)}, s32[8,832]{1,0:T(8,128)S(1)}, u32[]{:S(2)}) copy-start(s32[8,832]{1,0:T(8,128)S(1)} %reshape.54.refs_4_.refs_2_) | copy-start | bytes 79876
  29.9 16.5 %collective-permute-start.2 = (s32[8,832]{1,0:T(8,128)S(1)}, s32[8,832]{1,0:T(8,128)S(1)}, u32[]{:S(2)}, u32[]{:S(2)}) collective-permute-start(s32[8,832]{1,0:T(8,128)S(1)} %reshape.54.refs_4_.refs_2_), channel_id=1, source_target_pairs={{0,1},{1,0},{2,3},{3,2},{4,5},{5,4},{6,7},{7,6},{8,9},{9,8},{10,11... | collective-permute-start | bytes 79880 | tf_op jit(solution)/shard_map/ppermute | solution.py:927
  46.3 0.6 copy-start.5
  46.3 0.8 copy-start.1
  46.3 1.1 copy-start.2
